TPU v7x, 256 devices: a whole 4x4x8 slice. The times are simulated.
256 devices in a mesh: vocab: 32 (over y, z_lo, core), rep: 8 (over x, z_hi).
Axes of the slice: x: 4, y: 4, z: 8 (z_hi: 2, z_lo: 4; z = z_hi * 4 + z_lo), core: 2. Of those that a mesh axis runs over, the one named last changes fastest.
Arguments:
- src_ids: int32 [8, 256], P('rep'), may hold values from 0 to 131071
- tgt_ids: int32 [8, 128], P('rep'), may hold values from 0 to 131071
- tgt_mask: int32 [8, 128], P('rep'), may hold values from 0 to 1, as said below
- tgt_order: int32 [8, 128], P('rep'), may hold values from 0 to 127, each once within a row
- table: bfloat16 [131072, 1024], P('vocab'), may hold values from -0.6 to 0.6
- student_hidden: bfloat16 [8, 128, 1024], P('rep'), may hold values from -30 to 30
- teacher_hidden: bfloat16 [8, 128, 2048], P('rep', 'vocab'), may hold values from -25 to 25
- teacher_head: bfloat16 [131072, 2048], P('vocab', 'rep'), may hold values from -0.45 to 0.45
- src_embed_grad: bfloat16 [8, 256, 1024], P('rep'), may hold values from -0.4375 to 0.4375
- tgt_embed_grad: bfloat16 [8, 128, 1024], P('rep'), may hold values from -0.4375 to 0.4375
Outputs:
- src_embeds: bfloat16 [8, 256, 1024], P('rep', 'vocab')
- tgt_embeds: bfloat16 [8, 128, 1024], P('rep', 'vocab')
- kl_loss: float32 [], replicated
- hidden_grad: float32 [8, 128, 1024], P('rep', 'vocab')
- table_grad: bfloat16 [131072, 1024], P(('vocab', 'rep'))
Inputs may be any that keep to these rules, and one draw needn't show every extreme that they name: `tgt_mask`: each replica's mask is 1 on a prefix of at least 32 positions and 0 after it; in every draw one replica's mask is all ones. Row r lists every position of 0 to 127 once; teacher_hidden[r, j] is the teacher state of target position tgt_order[r, j].
All inputs are finite; a program needn't handle non-finite values.
Results may differ from a plain program's by a relative error of at most 0.0031.
Values may be sent and summed in bfloat16 or wider, within the bound.
A program may use at most 128 MiB of HBM per device.

v0:
```python
import math

import jax
import jax.numpy as jnp
from jax import lax
from jax.sharding import PartitionSpec as P


def contract_last(first, second):
    return lax.dot_general(
        first, second, (((1,), (1,)), ((), ())), preferred_element_type=jnp.float32
    )


def contract_first(first, second):
    return lax.dot_general(
        first, second, (((0,), (0,)), ((), ())), preferred_element_type=jnp.float32
    )


def on_device(
    src_ids,
    tgt_ids,
    tgt_mask,
    tgt_order,
    table,
    student_hidden,
    teacher_hidden,
    teacher_head,
    src_embed_grad,
    tgt_embed_grad,
):
    vocab_rows = table.shape[0]
    embed_scale = math.sqrt(table.shape[1])
    first_row = lax.axis_index("vocab") * vocab_rows
    src_local = src_ids[0] - first_row
    tgt_local = tgt_ids[0] - first_row

    def pick_rows(local_ids):
        inside = (local_ids >= 0) & (local_ids < vocab_rows)
        picked = jnp.take(table, jnp.clip(local_ids, 0, vocab_rows - 1), axis=0).astype(jnp.float32)
        return jnp.where(inside[:, None], picked, 0.0)[None]

    src_found, tgt_found = (
        lax.psum_scatter(
            pick_rows(src_local).astype(jnp.bfloat16), "vocab", scatter_dimension=1, tiled=True
        ).astype(jnp.float32),
        lax.psum_scatter(
            pick_rows(tgt_local).astype(jnp.bfloat16), "vocab", scatter_dimension=1, tiled=True
        ).astype(jnp.float32),
    )
    src_embeds = (src_found * embed_scale).astype(jnp.bfloat16)
    tgt_embeds = (tgt_found * embed_scale).astype(jnp.bfloat16)
    arrived = lax.all_gather(teacher_hidden, "vocab", axis=1, tiled=True)[0]
    ordered_states = jnp.zeros_like(arrived).at[tgt_order[0]].set(arrived)
    mask_float = tgt_mask[0].astype(jnp.float32)
    mask_total = lax.psum(jnp.sum(mask_float), "rep")
    slot_total = lax.axis_size("rep") * tgt_ids.shape[1]
    token_weight = mask_float * slot_total / mask_total
    hidden = student_hidden[0]
    student_logits = contract_last(hidden, table)
    block = ordered_states
    teacher_logits = contract_last(block, lax.all_gather(teacher_head, "rep", axis=1, tiled=True))
    student_top, teacher_top = lax.pmax(
        (jnp.max(student_logits, axis=1), jnp.max(teacher_logits, axis=1)), "vocab"
    )
    teacher_exp = jnp.exp(teacher_logits - teacher_top[:, None])
    own_student_sum = jnp.sum(jnp.exp(student_logits - student_top[:, None]), axis=1)
    own_teacher_sum = jnp.sum(teacher_exp, axis=1)
    own_cross = jnp.sum(teacher_exp * (teacher_logits - student_logits), axis=1)
    student_sum, teacher_sum, cross_sum = lax.psum(
        (own_student_sum, own_teacher_sum, own_cross), "vocab"
    )
    student_lse = student_top + jnp.log(student_sum)
    teacher_lse = teacher_top + jnp.log(teacher_sum)
    token_kl = cross_sum / teacher_sum - teacher_lse + student_lse
    kl_loss = lax.psum(jnp.sum(mask_float * token_kl), "rep") / mask_total
    student_prob = jnp.exp(student_logits - student_lse[:, None])
    teacher_prob = jnp.exp(teacher_logits - teacher_lse[:, None])
    logit_grad = (token_weight[:, None] * (student_prob - teacher_prob)).astype(jnp.bfloat16)
    block = logit_grad
    hidden_grad = lax.psum_scatter(
        jnp.dot(block, table, preferred_element_type=jnp.float32),
        "vocab",
        scatter_dimension=0,
        tiled=True,
    )[None]
    column_ids = lax.broadcasted_iota(jnp.int32, (1, vocab_rows), 1)
    src_onehot = (src_local[:, None] == column_ids).astype(jnp.bfloat16)
    tgt_onehot = (tgt_local[:, None] == column_ids).astype(jnp.bfloat16)
    left_side = jnp.concatenate([logit_grad, src_onehot, tgt_onehot], axis=0)
    src_scaled = (src_embed_grad[0].astype(jnp.float32) * embed_scale).astype(jnp.bfloat16)
    tgt_scaled = (tgt_embed_grad[0].astype(jnp.float32) * embed_scale).astype(jnp.bfloat16)
    right_side = jnp.concatenate([hidden, src_scaled, tgt_scaled], axis=0)
    block = left_side
    table_grad = lax.psum_scatter(
        contract_first(block, right_side), "rep", scatter_dimension=0, tiled=True
    ).astype(jnp.bfloat16)
    return (src_embeds, tgt_embeds, kl_loss, hidden_grad, table_grad)


def solution(mesh):
    return jax.shard_map(
        on_device,
        mesh=mesh,
        in_specs=(
            P("rep", None),
            P("rep", None),
            P("rep", None),
            P("rep", None),
            P("vocab", None),
            P("rep", None, None),
            P("rep", "vocab", None),
            P("vocab", "rep"),
            P("rep", None, None),
            P("rep", None, None),
        ),
        out_specs=(
            P("rep", "vocab", None),
            P("rep", "vocab", None),
            P(),
            P("rep", "vocab", None),
            P(("vocab", "rep"), None),
        ),
        check_vma=False,
    )
```

profile of v0, /device:TPU:32, one launch (start us, length us, event | category | flops | bytes accessed | tf_op | source)
XLA Modules:
  0.0 1308.6 jit_solution(2506005520698977467)
XLA Ops:
  8.8 5.5 gather_fusion.1
  15.4 6.0 gather_fusion
  21.4 1.0 select_convert_fusion
  22.6 1.9 fusion.6
  24.5 1.2 fusion.8
  25.7 65.5 %all_gather.6 = bf16[1,128,2048]{2,0,1:T(2,128)(2,1)S(1)} all-gather(bf16[1,4,2048]{2,0,1:T(2,128)(2,1)S(1)} %copy.16), channel_id=1, replica_groups=mesh['vocab'=32,'rep'=8] {'vocab'}, dimensions={1}, use_global_device_ids=true | all-gather | bytes 540672 | tf_op jit(solution)/shard_map/all_gather | solution.py:54
  91.3 6.6 fusion.27
  100.2 2.4 scatter_custom_fusion
  102.6 244.3 %all-gather.2.cloned.1.call-done = bf16[4096,2048]{1,0:T(8,128)(2,1)} async-done(((bf16[4096,256]{1,0:T(8,128)(2,1)}), bf16[4096,2048]{1,0:T(8,128)(2,1)}) %all-gather.2.cloned.1.call-update) | async-done | bytes 16777232 | tf_op jit(solution)/shard_map/all_gather | solution.py:63
  347.0 12.9 fusion.28
  359.9 63.5 %all-reduce.3 = (f32[128]{0:T(128)S(1)}, f32[128]{0:T(128)S(1)}) all-reduce(f32[128]{0:T(128)S(1)} %get-tuple-element.24, f32[128]{0:T(128)S(1)} %get-tuple-element.26), channel_id=1, replica_groups=mesh['vocab'=32,'rep'=8] {'vocab'}, use_global_device_ids=true, to_apply=%region_10.11 | all-reduce | flops 256 | bytes 2048 | tf_op jit(solution)/shard_map/pmax | solution.py:64
  423.4 2.5 multiply_reduce_fusion
  425.9 67.5 %all-reduce.2 = (f32[128]{0:T(128)S(1)}, f32[128]{0:T(128)S(1)}, f32[128]{0:T(128)S(1)}) all-reduce(f32[128]{0:T(128)S(1)} %get-tuple-element.7, f32[128]{0:T(128)S(1)} %get-tuple-element.6, f32[128]{0:T(128)S(1)} %get-tuple-element.5), channel_id=1, replica_groups=mesh['vocab'=32,'rep'=8] {'vocab'}, use_global_device_ids=true, to_apply=%region_12.13 | all-reduce | flops 384 | bytes 3072 | tf_op jit(solution)/shard_map/psum | solution.py:71
  494.0 26.5 %all-reduce.4 = (f32[]{:T(128)}, f32[]{:T(128)}) all-reduce(f32[]{:T(128)} %get-tuple-element.15, f32[]{:T(128)} %convert_reduce_fusion), channel_id=1, replica_groups=mesh['vocab'=32,'rep'=8] {'rep'}, use_global_device_ids=true, to_apply=%region_14.15 | all-reduce | flops 2 | bytes 16 | tf_op jit(solution)/shard_map/psum | solution.py:77
  521.2 2.3 multiply_convert_fusion
  523.5 5.6 fusion.29
  529.2 11.7 fusion
  542.9 1.3 multiply_convert_fusion.4
  544.2 114.8 %reduce-scatter.4.cloned.1.call-done = bf16[1,8,1024]{2,1,0:T(8,128)(2,1)} async-done(((bf16[1,256,1024]{2,1,0:T(8,128)(2,1)}), bf16[1,8,1024]{2,1,0:T(8,128)(2,1)}) %reduce-scatter.4.cloned.1.call-update) | async-done | bytes 16400 | tf_op jit(solution)/shard_map/reduce_scatter | solution.py:45
  659.0 1.3 multiply_convert_fusion.3
  661.6 271.8 %all-reduce.10.cloned.1.call-done = f32[128,1024]{1,0:T(8,128)} async-done(((f32[128,1024]{1,0:T(8,128)}), f32[128,1024]{1,0:T(8,128)}) %all-reduce.10.cloned.1.call-update) | async-done | bytes 524304
  933.5 1.4 dynamic-slice_bitcast_fusion
  934.8 362.3 %reduce-scatter.6.cloned.1.call-done = f32[512,1024]{1,0:T(8,128)} async-done(((f32[4096,1024]{1,0:T(8,128)}), f32[512,1024]{1,0:T(8,128)}) %reduce-scatter.6.cloned.1.call-update) | async-done | bytes 2097168 | tf_op jit(solution)/shard_map/reduce_scatter | solution.py:96
  1297.1 2.7 convert_element_type.115
  (47 shorter events, 6.8 us)
Async XLA Ops:
  8.0 0.8 copy-start.7
  8.0 339.0 %all-gather.2.cloned.1.call-start = ((), (), s32[]{:S(2)}) async-start(), calls=%async_computation.3 | async-start | bytes 18874368 | tf_op jit(solution)/shard_map/all_gather | solution.py:63
  8.7 6.6 copy-start.5
  8.8 534.1 %all-reduce.8.cloned.1.call-start = ((), (), s32[]{:S(2)}) async-start(), calls=%async_computation.5 | async-start | bytes 524288
  15.3 643.7 %reduce-scatter.4.cloned.1.call-start = ((), (), s32[]{:S(2)}) async-start(), calls=%async_computation.2 | async-start | bytes 540672 | tf_op jit(solution)/shard_map/reduce_scatter | solution.py:45
  22.5 3.3 copy-start.4
  22.5 68.8 %copy-start.8 = (s32[1,128]{1,0:T(1,128)S(1)}, s32[1,128]{1,0:T(1,128)}, u32[]{:S(2)}) copy-start(s32[1,128]{1,0:T(1,128)} %param.13) | copy-start | bytes 1540
  22.5 68.8 %copy-start.2 = (bf16[1,128,1024]{2,1,0:T(8,128)(2,1)S(1)}, bf16[1,128,1024]{2,1,0:T(8,128)(2,1)}, u32[]{:S(2)}) copy-start(bf16[1,128,1024]{2,1,0:T(8,128)(2,1)} %param.15) | copy-start | bytes 786436
  22.5 910.9 %all-reduce.10.cloned.1.call-start = ((), (), s32[]{:S(2)}) async-start(), calls=%async_computation.6 | async-start | bytes 1048576
  91.3 6.6 copy-start.6
  91.3 7.2 copy-start.1
  91.3 8.1 copy-start.3
  523.5 5.7 copy-start
  529.2 767.9 %reduce-scatter.6.cloned.1.call-start = ((), (), s32[]{:S(2)}) async-start(), calls=%async_computation.4 | async-start | bytes 18874368 | tf_op jit(solution)/shard_map/reduce_scatter | solution.py:96
  540.9 0.7 copy-start.9
Sparse Core Ops, SparseCore 0:
  11.3 335.6 all-gather.1
Sparse Core Ops, SparseCore 1:
  15.4 498.9 all-reduce.7
  516.9 142.1 reduce-scatter.3
  661.5 271.9 all-reduce.9
  938.3 358.7 reduce-scatter.5
where the time goes:
time: 1310 us
  waiting for transfers between devices  994 us (76%)
  blocking collectives  223 us (17%)
  matrix products  36.8 us (3%)
  between operations  19 us (1%)
  other arithmetic  18.8 us (1%)
  local copies, waits for them, and re-layouts  16.6 us (1%)
    reduce_scatter x1, waiting for transfers between devices, on_device(): lax.psum_scatter(contract_first(block, right_side), 'rep', scatter_dimens...  362 us
    unnamed x7, waiting for transfers between devices  273 us
    all_gather x1, waiting for transfers between devices, on_device(): lax.all_gather(teacher_head, 'rep', axis=1, tiled=True)  244 us
    reduce_scatter x1, waiting for transfers between devices, on_device(): lax.psum_scatter(pick_rows(src_local).astype(jnp.bfloat16), 'vocab', scat...  115 us
    psum x1, blocking collectives, on_device(): lax.psum((own_student_sum, own_teacher_sum, own_cross), 'vocab')  67.5 us
    all_gather x1, blocking collectives, on_device(): arrived = lax.all_gather(teacher_hidden, 'vocab', axis=1, tiled=True)[0]  65.5 us
    pmax x1, blocking collectives, on_device(): lax.pmax((jnp.max(student_logits, axis=1), jnp.max(teacher_logits, axis=1...  63.5 us
    psum x1, blocking collectives, on_device(): kl_loss = lax.psum(jnp.sum(mask_float * token_kl), 'rep') / mask_total  26.5 us
  transfers between devices with their start and end apart: 5, of which 4 were waited for; matrix products, arithmetic and copies ran while one was open for 5% of the time, Pallas kernels for 0%

commit v1 on v0

v1 whole, which is shorter than its diff:
```python
import functools
import math

import jax
import jax.numpy as jnp
from jax import lax
from jax.experimental import pallas as pl
from jax.experimental.pallas import tpu as pltpu
from jax.sharding import PartitionSpec as P

MESH = pl.DeviceIdType.MESH
NX, NY, NZL, NZH, NC = 4, 4, 4, 2, 2
NZ = NZL * NZH
F32, BF16 = jnp.float32, jnp.bfloat16


def dot_nt(a, b):
    return lax.dot_general(a, b, (((1,), (1,)), ((), ())), preferred_element_type=F32)


def dot_nn(a, b):
    return lax.dot_general(a, b, (((1,), (0,)), ((), ())), preferred_element_type=F32)


def dot_tn(a, b):
    return lax.dot_general(a, b, (((0,), (0,)), ((), ())), preferred_element_type=F32)


def merge(own, others):
    groups = own.shape[0] // 4
    tops = [piece[0:4] for piece in [own] + others]
    top = functools.reduce(jnp.maximum, tops)
    total = [0.0] * (groups - 1)
    for piece, piece_top in zip([own] + others, tops):
        factor = jnp.exp(piece_top - top)
        for g in range(1, groups):
            total[g - 1] = total[g - 1] + piece[4 * g : 4 * g + 4] * factor
    return jnp.concatenate([top] + total, axis=0)


def kernel(
    head, table, hidden_in, src_cot, tgt_cot, states_in, meta_in, ids_col,
    emb_out, kl_out, hg_out, tg_out,
    tab, headbuf, hid, cot, st, meta, order_st, slog, tlog, acc, gbuf, gx,
    emb, emb_2, emb_c, emb_y, emb_z,
    sstat, sst_c, sst_x, sst_y, sst_z, tstat, tst_c, tst_x, tst_y, tst_z,
    hp, hp_c, h1, h1_y, h2, h2_z,
    lsem, ssem, rsem,
):
    v, r = lax.axis_index("vocab"), lax.axis_index("rep")
    y, zl, c = v // 8, (v // 2) % 4, v % 2
    x, zh = r // 2, r % 2
    z = zh * 4 + zl
    oc = 1 - c
    oz = 1 - zh

    def dev(y=y, zl=zl, c=c, x=x, zh=zh):
        return ((y * 4 + zl) * 2 + c, x * 2 + zh)

    def zdev(d):
        to = (z + d) % 8
        return dev(zl=to % 4, zh=to // 4)

    used = {"l": 0, "r": 0}
    pending = []

    def local(src, dst):
        i = used["l"]
        used["l"] += 1
        copy = pltpu.make_async_copy(src, dst, lsem.at[i])
        copy.start()
        return copy

    def send(src, dst, to):
        i = used["r"]
        used["r"] += 1
        copy = pltpu.make_async_remote_copy(
            src_ref=src, dst_ref=dst, send_sem=ssem.at[i], recv_sem=rsem.at[i],
            device_id=to, device_id_type=MESH,
        )
        copy.start()
        pending.append(copy)
        return copy

    def arrive(copies):
        for copy in copies:
            copy.wait_recv()

    tab_copies = [local(table.at[pl.ds(b * 512, 512)], tab.at[b]) for b in range(8)]
    st_rows = pl.ds(pl.multiple_of(c * 256 + y * 64 + zl * 16, 16), 16)
    st_rows_y = pl.ds(pl.multiple_of(c * 256 + y * 64, 64), 64)
    st_rows_c = pl.ds(pl.multiple_of(c * 256, 256), 256)
    own_st = local(states_in, st.at[:, x, zh, st_rows, :])
    own_hid = local(hidden_in, hid.at[x, zh])
    own_meta = local(meta_in, meta.at[x, zh])
    own_cot = [
        local(src_cot, cot.at[x, zh, pl.ds(0, 256)]),
        local(tgt_cot, cot.at[x, zh, pl.ds(256, 128)]),
    ]
    own_head = local(head.at[pl.ds(pl.multiple_of(r * 512, 512), 512)], headbuf.at[r])

    own_hid.wait()
    for copy in own_cot:
        copy.wait()

    barrier = pltpu.get_barrier_semaphore()
    rep_offsets = [(dx, dz) for dz in (0, 1) for dx in range(4) if (dx, dz) != (0, 0)]
    peers = [dev(x=(x + dx) % 4, zh=(zh + dz) % 2) for dx, dz in rep_offsets]
    peers += [zdev(d) for d in range(1, 8) if d != 4]
    peers += [dev(y=(y + d) % 4) for d in range(1, 4)]
    peers += [dev(c=oc)]
    for peer in peers:
        pl.semaphore_signal(barrier, inc=1, device_id=peer, device_id_type=MESH)
    pl.semaphore_wait(barrier, len(peers))

    own_st.wait()
    st_z = [
        send(st.at[:, x, zh, st_rows, :], st.at[:, x, zh, st_rows, :], zdev(d)) for d in range(1, 8)
    ]
    own_meta.wait()
    meta_r = [
        send(meta.at[x, zh], meta.at[x, zh], dev(x=(x + dx) % 4, zh=(zh + dz) % 2))
        for dx, dz in rep_offsets
    ]
    hid_8th = pl.ds(pl.multiple_of(c * 64 + y * 16, 16), 16)
    hid_half = pl.ds(pl.multiple_of(c * 64, 64), 64)
    hid_z = [send(hid.at[x, zh, hid_8th], hid.at[x, zh, hid_8th], dev(zh=oz))]
    head_r = []
    for dx, dz in rep_offsets[3:] + rep_offsets[:3]:
        to_x, to_zh = (x + dx) % 4, (zh + dz) % 2
        rows = pl.ds(pl.multiple_of((to_x * 2 + to_zh) * 512, 512), 512)
        head_r.append(send(head.at[rows], headbuf.at[r], dev(x=to_x, zh=to_zh)))
    head_z, head_x = head_r[:4], head_r[4:]
    cot_8th = pl.ds(pl.multiple_of(c * 192 + y * 48, 16), 48)
    cot_half = pl.ds(pl.multiple_of(c * 192, 64), 192)
    cot_z = [send(cot.at[x, zh, cot_8th], cot.at[x, zh, cot_8th], dev(zh=oz))]

    for copy in tab_copies:
        copy.wait()
    lane = lax.broadcasted_iota(jnp.int32, (512, 512), 1)

    def emb_part(b, carry):
        onehot = (ids_col[...] == lane + b * 512).astype(BF16)
        part = dot_nn(onehot, tab[b])

        @pl.when(b == 0)
        def _():
            acc[...] = part

        @pl.when(b != 0)
        def _():
            acc[...] += part

        return carry

    lax.fori_loop(0, 2, emb_part, 0)
    arrive(st_z)
    st_y = [
        send(st.at[:, x, :, st_rows_y, :], st.at[:, x, :, st_rows_y, :], dev(y=(y + d) % 4))
        for d in range(1, 4)
    ]
    arrive(hid_z)
    hid_x = [
        send(hid.at[x, :, hid_8th, :], hid.at[x, :, hid_8th, :], dev(x=(x + d) % 4))
        for d in range(1, 4)
    ]
    lax.fori_loop(2, 4, emb_part, 0)
    arrive(st_y)
    st_x = [
        send(st.at[:, x, :, st_rows_c, :], st.at[:, x, :, st_rows_c, :], dev(x=(x + d) % 4))
        for d in range(1, 4)
    ]
    arrive(hid_x)
    hid_y = [
        send(hid.at[:, :, hid_8th, :], hid.at[:, :, hid_8th, :], dev(y=(y + d) % 4))
        for d in range(1, 4)
    ]
    cot_own_x = [
        send(cot.at[x, zh, cot_half], cot.at[x, zh, cot_half], dev(x=(x + d) % 4))
        for d in range(1, 4)
    ]
    arrive(cot_z)
    cot_far_x = [
        send(cot.at[x, oz, cot_8th], cot.at[x, oz, cot_8th], dev(x=(x + d) % 4))
        for d in range(1, 4)
    ]
    lax.fori_loop(4, 8, emb_part, 0)
    emb[...] = acc[...].astype(BF16).reshape(2, 256, 1024)
    emb_cs = [send(emb.at[oc], emb_c, dev(c=oc))]
    arrive(hid_y)
    hid_c = [send(hid.at[:, :, hid_half, :], hid.at[:, :, hid_half, :], dev(c=oc))]
    arrive(st_x)
    st_c = [send(st.at[:, :, :, st_rows_c, :], st.at[:, :, :, st_rows_c, :], dev(c=oc))]
    arrive(emb_cs)
    emb_1 = (emb[c].astype(F32) + emb_c[...].astype(F32)).astype(BF16)
    emb[c] = emb_1
    emb_ys = [
        send(
            emb.at[c, pl.ds(pl.multiple_of(((y + d) % 4) * 64, 64), 64)],
            emb_y.at[d - 1], dev(y=(y + d) % 4),
        )
        for d in range(1, 4)
    ]
    arrive(cot_far_x)
    cot_y = [
        send(cot.at[:, oz, cot_8th, :], cot.at[:, oz, cot_8th, :], dev(y=(y + d) % 4))
        for d in range(1, 4)
    ]

    arrive(hid_c)
    own_rows = tab.at[r]

    def student(p, carry):
        slog[p] = dot_nt(own_rows[...], hid[p].reshape(256, 1024))
        return carry

    lax.fori_loop(0, 4, student, 0)
    for p in range(4):
        values = slog[p]
        top = jnp.max(values, axis=0, keepdims=True)
        sstat[0, p : p + 1, :] = top
        sstat[0, 4 + p : 5 + p, :] = jnp.sum(jnp.exp(values - top), axis=0, keepdims=True)
    sst_cs = [send(sstat.at[0], sst_c, dev(c=oc))]

    arrive(emb_ys)
    mine = emb[c, pl.ds(pl.multiple_of(y * 64, 64), 64)].astype(F32)
    for d in range(3):
        mine = mine + emb_y[d].astype(F32)
    emb_2[...] = mine.astype(BF16)
    emb_zs = [
        send(
            emb_2.at[pl.ds(pl.multiple_of(((zl + d) % 4) * 16, 16), 16)],
            emb_z.at[d - 1], dev(zl=(zl + d) % 4),
        )
        for d in range(1, 4)
    ]

    arrive(sst_cs)
    sstat[1] = merge(sstat[0], [sst_c[...]])
    sst_xs = [send(sstat.at[1], sst_x.at[d - 1], dev(x=(x + d) % 4)) for d in range(1, 4)]

    arrive(st_c)
    arrive(meta_r)
    slot = lax.broadcasted_iota(jnp.int32, (512, 128), 0)
    lane_128 = lax.broadcasted_iota(jnp.int32, (512, 128), 1)

    def place(i, carry):
        px, pz = i // 2, i % 2
        rows = meta[px, pz]
        parts = [
            ((rows[4 + k : 5 + k, :] == slot % 128) & (lane_128 % 4 == slot // 128)).astype(BF16)
            for k in range(4)
        ]
        move = jnp.concatenate(parts, axis=1)
        for half in range(2):
            placed = dot_nn(move, st[half, px, pz]).astype(BF16)
            for j in range(4):
                order_st[half * 4 + j, px, pz] = placed[j * 128 : (j + 1) * 128]
        return carry

    lax.fori_loop(0, 8, place, 0)

    arrive(sst_xs)
    sstat[2] = merge(sstat[1], [sst_x[d] for d in range(3)])
    sst_ys = [send(sstat.at[2], sst_y.at[d - 1], dev(y=(y + d) % 4)) for d in range(1, 4)]

    def teacher(chunk, first):
        def one(p, carry):
            part = dot_nt(headbuf[chunk], order_st[chunk, p].reshape(256, 256))
            if first:
                tlog[p] = part
            else:
                tlog[p] += part
            return carry

        lax.fori_loop(0, 4, one, 0)

    own_head.wait()
    teacher(r, True)
    arrive(sst_ys)
    sstat[3] = merge(sstat[2], [sst_y[d] for d in range(3)])
    sst_zs = [send(sstat.at[3], sst_z.at[d - 1], zdev(d)) for d in range(1, 8)]
    for k, d in enumerate(range(1, 4)):
        head_x[k].wait_recv()
        teacher(((x + 4 - d) % 4) * 2 + zh, False)

    arrive(cot_own_x)
    arrive(cot_y)
    cot_c = [send(cot.at[:, :, cot_half, :], cot.at[:, :, cot_half, :], dev(c=oc))]

    arrive(emb_zs)
    mine = emb_2[pl.ds(pl.multiple_of(zl * 16, 16), 16)].astype(F32)
    for d in range(3):
        mine = mine + emb_z[d].astype(F32)
    emb_out[...] = (mine * 32.0).astype(BF16)

    for k, d in enumerate(range(0, 4)):
        head_z[k].wait_recv()
        teacher(((x + 4 - d) % 4) * 2 + oz, False)

    for p in range(4):
        values = tlog[p]
        top = jnp.max(values, axis=0, keepdims=True)
        weights = jnp.exp(values - top)
        tstat[0, p : p + 1, :] = top
        tstat[0, 4 + p : 5 + p, :] = jnp.sum(weights, axis=0, keepdims=True)
        tstat[0, 8 + p : 9 + p, :] = jnp.sum(weights * (values - slog[p]), axis=0, keepdims=True)
        tstat[0, 12 + p : 13 + p, :] = jnp.zeros((1, 256), F32)
    tst_cs = [send(tstat.at[0], tst_c, dev(c=oc))]
    arrive(sst_zs)
    student_total = merge(sstat[3], [sst_z[d] for d in range(7)])
    student_lse = student_total[0:4] + jnp.log(student_total[4:8])
    mask = jnp.concatenate(
        [
            jnp.concatenate([meta[p, 0, 3:4, :], meta[p, 1, 3:4, :]], axis=1).astype(F32)
            for p in range(4)
        ],
        axis=0,
    )
    mask_total = jnp.sum(mask, axis=(0, 1), keepdims=True)
    token_weight = mask * (8 * 128) / mask_total
    arrive(tst_cs)
    tstat[1] = merge(tstat[0], [tst_c[...]])
    tst_xs = [send(tstat.at[1], tst_x.at[d - 1], dev(x=(x + d) % 4)) for d in range(1, 4)]
    arrive(tst_xs)
    tstat[2] = merge(tstat[1], [tst_x[d] for d in range(3)])
    tst_ys = [send(tstat.at[2], tst_y.at[d - 1], dev(y=(y + d) % 4)) for d in range(1, 4)]
    arrive(tst_ys)
    tstat[3] = merge(tstat[2], [tst_y[d] for d in range(3)])
    tst_zs = [send(tstat.at[3], tst_z.at[d - 1], zdev(d)) for d in range(1, 8)]
    arrive(tst_zs)
    total = merge(tstat[3], [tst_z[d] for d in range(7)])
    teacher_sum = total[4:8]
    teacher_lse = total[0:4] + jnp.log(teacher_sum)

    sstat[4, 0:4, :] = student_lse
    sstat[4, 4:8, :] = token_weight
    tstat[4, 0:4, :] = teacher_lse

    def gradient(p):
        row = pl.ds(p, 1)
        student_prob = jnp.exp(slog[p] - sstat[4, row, :])
        teacher_prob = jnp.exp(tlog[p] - tstat[4, row, :])
        return (sstat[4, pl.ds(4 + p, 1), :] * (student_prob - teacher_prob)).astype(BF16)

    g_x = []
    for d in range(1, 4):
        p = (x + d) % 4
        gbuf[p] = gradient(p)
        g_x.append(send(gbuf.at[p], gx.at[x], dev(x=p)))
    own_grad = gradient(x)
    gbuf[x] = own_grad
    gx[x] = own_grad

    token_kl = total[8:12] / teacher_sum - teacher_lse + student_lse
    kl = jnp.sum(mask * token_kl, axis=(0, 1), keepdims=True) / mask_total
    kl_out[...] = jnp.broadcast_to(kl, (8, 128))

    def hidden_part(k, first):
        part = dot_tn(gx[k], tab[k * 2 + zh]).reshape(2, 2, 64, 1024)
        if first:
            hp[...] = part
        else:
            hp[...] += part

    hidden_part(x, True)
    for d in range(1, 4):
        g_x[d - 1].wait_recv()
        hidden_part((x + 4 - d) % 4, False)
    hp_cs = [send(hp.at[:, oc], hp_c, dev(c=oc))]

    def table_part(p, carry):
        part = dot_nn(gbuf[p], hid[p].reshape(256, 1024))

        @pl.when(p == 0)
        def _():
            acc[...] = part

        @pl.when(p != 0)
        def _():
            acc[...] += part

        return carry

    lax.fori_loop(0, 4, table_part, 0)
    arrive(hp_cs)
    h1[...] = (hp[:, c] + hp_c[...]).reshape(2, 4, 16, 1024)
    h1_ys = [
        send(h1.at[:, (y + d) % 4], h1_y.at[d - 1], dev(y=(y + d) % 4)) for d in range(1, 4)
    ]

    arrive(cot_c)
    base = v * 4096 + r * 512

    def lookup(i, carry):
        px, pz = i // 2, i % 2
        rows = meta[px, pz]
        onehot = jnp.concatenate(
            [(rows[k : k + 1, :] - base == slot).astype(BF16) for k in range(3)], axis=1
        )
        acc[...] += dot_nn(onehot, cot[px, pz]) * 32.0
        return carry

    lax.fori_loop(0, 4, lookup, 0)
    arrive(h1_ys)
    mine = h1[:, y]
    for d in range(3):
        mine = mine + h1_y[d]
    for i in range(4):
        h2[:, i] = mine[:, 4 * i : 4 * i + 4]
    h2_zs = []
    for d in range(1, 8):
        to = (z + d) % 8
        h2_zs.append(send(h2.at[to // 4, to % 4], h2_z.at[d - 1], zdev(d)))
    lax.fori_loop(4, 8, lookup, 0)
    tg_out[...] = acc[...].astype(BF16)
    arrive(h2_zs)
    result = h2[zh, zl]
    for d in range(7):
        result = result + h2_z[d]
    hg_out[...] = result
    for copy in pending:
        copy.wait_send()


def on_device(
    src_ids, tgt_ids, tgt_mask, tgt_order, table, student_hidden, teacher_hidden, teacher_head,
    src_embed_grad, tgt_embed_grad,
):
    first_row = lax.axis_index("vocab") * table.shape[0]

    def slots(values, n):
        return values.reshape((4, 4, 2, n) + values.shape[1:]).swapaxes(1, 2).swapaxes(0, 1)

    hidden = slots(student_hidden[0], 4).reshape(128, 1024)
    mask = slots(tgt_mask[0], 4).reshape(1, 128)
    order = slots(tgt_order[0], 4).reshape(128)
    order = (order // 4) % 2 * 64 + order // 32 * 16 + (order // 8) % 4 * 4 + order % 4
    order = jnp.repeat(order, 4).reshape(4, 128)
    meta = jnp.concatenate([src_ids[0].reshape(2, 128), tgt_ids, mask, order], axis=0)
    ids_col = jnp.concatenate(
        [
            slots(src_ids[0], 8) - first_row,
            slots(tgt_ids[0], 4) - first_row,
            jnp.full((2, 4, 4, 4), -1, jnp.int32),
        ],
        axis=3,
    ).reshape(512, 1)
    states = teacher_hidden[0].reshape(4, 2, 4, 256).swapaxes(0, 1).reshape(2, 16, 256)

    vmem = pl.BlockSpec(memory_space=pltpu.VMEM)
    hbm = pl.BlockSpec(memory_space=pl.ANY)

    def scratch(shape, dtype=BF16):
        return pltpu.VMEM(shape, dtype)

    emb, kl, hg, tg = pl.pallas_call(
        kernel,
        name="distill",
        out_shape=(
            jax.ShapeDtypeStruct((16, 1024), BF16),
            jax.ShapeDtypeStruct((8, 128), F32),
            jax.ShapeDtypeStruct((4, 1024), F32),
            jax.ShapeDtypeStruct((512, 1024), BF16),
        ),
        in_specs=[hbm, hbm, hbm, hbm, hbm, hbm, hbm, vmem],
        out_specs=(vmem, vmem, vmem, vmem),
        scratch_shapes=[
            scratch((8, 512, 1024)),
            scratch((8, 512, 256)),
            scratch((4, 2, 128, 1024)),
            scratch((4, 2, 384, 1024)),
            scratch((2, 4, 2, 512, 256)),
            scratch((4, 2, 8, 128), jnp.int32),
            scratch((8, 4, 2, 128, 256)),
            scratch((4, 512, 256), F32),
            scratch((4, 512, 256), F32),
            scratch((512, 1024), F32),
            scratch((4, 512, 256)),
            scratch((4, 512, 256)),
            scratch((2, 256, 1024)),
            scratch((64, 1024)),
            scratch((256, 1024)),
            scratch((3, 64, 1024)),
            scratch((3, 16, 1024)),
            scratch((5, 8, 256), F32),
            scratch((8, 256), F32),
            scratch((3, 8, 256), F32),
            scratch((3, 8, 256), F32),
            scratch((7, 8, 256), F32),
            scratch((5, 16, 256), F32),
            scratch((16, 256), F32),
            scratch((3, 16, 256), F32),
            scratch((3, 16, 256), F32),
            scratch((7, 16, 256), F32),
            scratch((2, 2, 64, 1024), F32),
            scratch((2, 64, 1024), F32),
            scratch((2, 4, 16, 1024), F32),
            scratch((3, 2, 16, 1024), F32),
            scratch((2, 4, 4, 1024), F32),
            scratch((7, 4, 1024), F32),
            pltpu.SemaphoreType.DMA((16,)),
            pltpu.SemaphoreType.DMA((112,)),
            pltpu.SemaphoreType.DMA((112,)),
        ],
        compiler_params=pltpu.CompilerParams(
            collective_id=0, has_side_effects=True, vmem_limit_bytes=60 * 2**20
        ),
        cost_estimate=pl.CostEstimate(
            flops=12 * 10**9, bytes_accessed=16 * 2**20, transcendentals=2 * 10**6
        ),
    )(
        teacher_head, table, hidden, src_embed_grad[0], tgt_embed_grad[0], states, meta, ids_col,
    )
    return (emb[None, 0:8], emb[None, 8:12], kl[0, 0], hg[None], tg)


def solution(mesh):
    return jax.shard_map(
        on_device,
        mesh=mesh,
        in_specs=(
            P("rep", None),
            P("rep", None),
            P("rep", None),
            P("rep", None),
            P("vocab", None),
            P("rep", None, None),
            P("rep", "vocab", None),
            P("vocab", "rep"),
            P("rep", None, None),
            P("rep", None, None),
        ),
        out_specs=(
            P("rep", "vocab", None),
            P("rep", "vocab", None),
            P(),
            P("rep", "vocab", None),
            P(("vocab", "rep"), None),
        ),
        check_vma=False,
    )
```

time: 1310 us -> 186 us (0.14)
  waiting for transfers between devices: 994 us -> 0 us
  blocking collectives: 223 us -> 0 us
  Pallas kernels: 0 us -> 167 us
  matrix products: 36.8 us -> 0 us
  between operations: 19 us -> 0.74 us
  other arithmetic: 18.8 us -> 5.41 us
    reduce_scatter x2 -> x0, waiting for transfers between devices: 477 us -> none  [the longest x1 362 us: on_device(): lax.psum_scatter(contract_first(block, right_side), 'rep', scatter_dimens...]
    unnamed x7 -> x0, waiting for transfers between devices: 273 us -> none
    all_gather x1 -> x0, waiting for transfers between devices: 244 us -> none  [on_device(): lax.all_gather(teacher_head, 'rep', axis=1, tiled=True)]
    pallas_call x0 -> x1, Pallas kernels: none -> 167 us  [on_device(): pl.pallas_call(kernel, name='distill', out_shape=(jax.ShapeDtypeStruct((1...]
    psum x2 -> x0, blocking collectives: 94 us -> none  [the longest x1 67.5 us: on_device(): lax.psum((own_student_sum, own_teacher_sum, own_cross), 'vocab')]
    all_gather x1 -> x0, blocking collectives: 65.5 us -> none  [on_device(): arrived = lax.all_gather(teacher_hidden, 'vocab', axis=1, tiled=True)[0]]
    pmax x1 -> x0, blocking collectives: 63.5 us -> none  [on_device(): lax.pmax((jnp.max(student_logits, axis=1), jnp.max(teacher_logits, axis=1...]
    dot_general x4 -> x0, matrix products: 36.8 us -> none  [the longest x2 19.5 us: contract_last(): lax.dot_general(first, second, (((1,), (1,)), ((), ())), preferred_elemen...]
  transfers between devices with their start and end apart: 5 -> 0, of which waited for: 4 -> 0; matrix products, arithmetic and copies ran while one was open for 5% -> 0% of each run, Pallas kernels for 0% -> 0%
where the time goes in v1:
time: 186 us
  Pallas kernels  167 us (90%)
  local copies, waits for them, and re-layouts  13 us (7%)
  other arithmetic  5.41 us (3%)
    pallas_call x1, Pallas kernels, on_device(): pl.pallas_call(kernel, name='distill', out_shape=(jax.ShapeDtypeStruct((1...  167 us
    unnamed x3, local copies, waits for them, and re-layouts  4.1 us

profile of v1, /device:TPU:32, one launch (start us, length us, event | category | flops | bytes accessed | tf_op | source)
XLA Modules:
  0.0 185.9 jit_solution(5910901674449041965)
XLA Ops:
  0.6 0.5 broadcast.84
  1.1 1.3 reduce.15
  2.5 1.3 reduce.14
  3.8 0.7 subtract_reduce_fusion.1
  4.5 0.7 subtract_reduce_fusion
  5.2 0.1 sub.43
  5.3 0.1 sub.47
  5.6 0.1 reshape_squeeze.21
  5.8 0.1 reshape_squeeze.20
  5.9 0.1 reshape.34
  6.1 0.7 reshape_squeeze.18
  6.8 0.6 reshape.33.states_in
  7.5 0.1 broadcast_in_dim.18
  7.6 1.3 pad_add_fusion.meta_in
  8.9 0.9 reshape.37.ids_col
  9.8 1.1 reshape_squeeze.17
  10.9 0.1 copy.31
  11.0 0.8 reshape.32.hidden_in
  11.7 166.7 %distill.1 = (bf16[16,1024]{1,0:T(8,128)(2,1)}, f32[8,128]{1,0:T(8,128)}, f32[4,1024]{1,0:T(4,128)}, bf16[512,1024]{1,0:T(8,128)(2,1)}) custom-call(bf16[4096,256]{1,0:T(8,128)(2,1)} %head.1, bf16[4096,1024]{1,0:T(8,128)(2,1)} %table.1, bf16[128,1024]{1,0:T(8,128)(2,1)} %reshape.32.hidden_in, bf16[256,1024]{1,0:T(8,128)(2,1)} %bitcast.29, ...), custom_call_target="tpu_custom_call" | custom-call | flops 12000000000 | bytes 16777216 | tf_op jit(solution)/shard_map/distill/pallas_call | solution.py:457
  178.5 1.2 slice.11
  179.7 1.3 slice_bitcast_fusion.1
  181.0 1.3 slice_bitcast_fusion
  182.3 1.3 copy.36
  183.6 2.3 %copy.37 = bf16[512,1024]{1,0:T(8,128)(2,1)} copy(bf16[512,1024]{1,0:T(8,128)(2,1)} %get-tuple-element.22) | data formatting | bytes 2097152
  (11 shorter events, 0.4 us)

commit v2 on v1

v2 whole, which is shorter than its diff:
```python
import functools

import jax
import jax.numpy as jnp
from jax import lax
from jax.experimental import pallas as pl
from jax.experimental.pallas import tpu as pltpu
from jax.sharding import PartitionSpec as P

MESH = pl.DeviceIdType.MESH
PACK = 16
NX, NY, NZL, NZH, NC = 4, 4, 4, 2, 2
NZ = NZL * NZH
F32, BF16 = jnp.float32, jnp.bfloat16


def dot_nt(a, b):
    return lax.dot_general(a, b, (((1,), (1,)), ((), ())), preferred_element_type=F32)


def dot_nn(a, b):
    return lax.dot_general(a, b, (((1,), (0,)), ((), ())), preferred_element_type=F32)


def dot_tn(a, b):
    return lax.dot_general(a, b, (((0,), (0,)), ((), ())), preferred_element_type=F32)


def merge(own, others):
    groups = own.shape[0] // 4
    tops = [piece[0:4] for piece in [own] + others]
    top = functools.reduce(jnp.maximum, tops)
    total = [0.0] * (groups - 1)
    for piece, piece_top in zip([own] + others, tops):
        factor = jnp.exp(piece_top - top)
        for g in range(1, groups):
            total[g - 1] = total[g - 1] + piece[4 * g : 4 * g + 4] * factor
    return jnp.concatenate([top] + total, axis=0)


def kernel(
    head, table, hidden_in, src_cot, tgt_cot, states_in, src_ids, tgt_ids, tgt_mask, tgt_order,
    src_out, tgt_out, kl_out, hg_out, full_out, base, packs, meta,
    tab, headbuf, hid_raw, hid, cot, pack, st, st_f32, expand, slot_ids, order_st, slog, tlog,
    acc, gbuf, gx, emb, emb_2, emb_c, emb_y, emb_z,
    sstat, sst_1, sst_2, sst_3, tstat, tst_1, tst_2, tst_3, cstat, cst_1, cst_2, cst_3,
    hp, hp_c, h1, h1_y, h2, h2_z,
    lsem, ssem, rsem,
):
    v, r = lax.axis_index("vocab"), lax.axis_index("rep")
    y, zl, c = v // 8, (v // 2) % 4, v % 2
    x, zh = r // 2, r % 2
    z = zh * 4 + zl
    oc = 1 - c
    oz = 1 - zh

    def dev(y=y, zl=zl, c=c, x=x, zh=zh):
        return ((y * 4 + zl) * 2 + c, x * 2 + zh)

    def zdev(d):
        to = (z + d) % 8
        return dev(zl=to % 4, zh=to // 4)

    def xdev(d):
        return dev(x=(x + d) % 4)

    def ydev(d):
        return dev(y=(y + d) % 4)

    def xcdev(dx, dc):
        return dev(x=(x + dx) % 4, c=(c + dc) % 2)

    used = {"l": 0, "r": 0}
    pending = []

    def local(src, dst):
        i = used["l"]
        used["l"] += 1
        copy = pltpu.make_async_copy(src, dst, lsem.at[i])
        copy.start()
        return copy

    def send(src, dst, to):
        i = used["r"]
        used["r"] += 1
        copy = pltpu.make_async_remote_copy(
            src_ref=src, dst_ref=dst, send_sem=ssem.at[i], recv_sem=rsem.at[i],
            device_id=to, device_id_type=MESH,
        )
        copy.start()
        pending.append(copy)
        return copy

    def same(ref, to):
        return send(ref, ref, to)

    def arrive(copies):
        for copy in copies:
            copy.wait_recv()

    barrier = pltpu.get_barrier_semaphore()
    rep_offsets = [(dx, dz) for dz in (1, 0) for dx in range(4) if (dx, dz) != (0, 0)]
    xc_offsets = [(dx, dc) for dc in (0, 1) for dx in range(4) if (dx, dc) != (0, 0)]
    peers = [dev(x=(x + dx) % 4, zh=(zh + dz) % 2) for dx, dz in rep_offsets]
    peers += [zdev(d) for d in range(1, 8) if d != 4]
    peers += [ydev(d) for d in range(1, 4)]
    peers += [xcdev(dx, 1) for dx in range(4)]
    for peer in peers:
        pl.semaphore_signal(barrier, inc=1, device_id=peer, device_id_type=MESH)

    def rows(start, step, count):
        return pl.ds(pl.multiple_of(start, step), count)

    own_raw = local(hidden_in.at[0], hid_raw)
    own_head = local(head.at[rows(r * 512, 512, 512)], headbuf.at[r])
    own_cot = [
        local(src_cot.at[0], cot.at[pl.ds(0, 256)]),
        local(tgt_cot.at[0], cot.at[pl.ds(256, 128)]),
    ]
    tab_copies = [local(table.at[pl.ds(b * 512, 512)], tab.at[b]) for b in range(8)]

    st_8th = rows(c * 256 + y * 64 + zl * 16, 16, 16)
    st_y = rows(c * 256 + y * 64, 64, 64)
    st_c = rows(c * 256, 256, 256)
    for k in range(8):
        st_f32[k // 4, (k % 4) * 4 : (k % 4) * 4 + 4, :] = states_in[
            0, :, k * 256 : (k + 1) * 256
        ].astype(F32)
    for half in range(2):
        st[half, x, zh, st_8th, :] = st_f32[half].astype(BF16)
    own_slot = c * 64 + y * 16 + lax.broadcasted_iota(jnp.int32, (16, 128), 0)

    def position(s):
        return (s // 16) % 4 * 32 + (s // 4) % 4 * 8 + s // 64 * 4 + s % 4

    pick = (position(own_slot) == lax.broadcasted_iota(jnp.int32, (16, 128), 1)).astype(BF16)
    hid_8th = rows(c * 64 + y * 16, 16, 16)
    hid_half = rows(c * 64, 64, 64)
    own_raw.wait()
    hid[x, zh, hid_8th, :] = dot_nn(pick, hid_raw[...]).astype(BF16)

    pl.semaphore_wait(barrier, len(peers))

    st_zs = [same(st.at[:, x, zh, st_8th, :], zdev(d)) for d in range(1, 8)]
    hid_z = [same(hid.at[x, zh, hid_8th], dev(zh=oz))]

    def send_head(offsets):
        copies = []
        for dx, dz in offsets:
            to_x, to_zh = (x + dx) % 4, (zh + dz) % 2
            block = head.at[rows((to_x * 2 + to_zh) * 512, 512, 512)]
            copies.append(send(block, headbuf.at[r], dev(x=to_x, zh=to_zh)))
        return copies

    head_x = send_head(rep_offsets[4:])

    ids = jnp.concatenate([src_ids[...], tgt_ids[...]], axis=1)
    pieces = jnp.concatenate(
        [ids & 255, (ids >> 8) & 255, ids >> 16, jnp.zeros((13, 384), jnp.int32)], axis=0
    ).astype(F32).astype(BF16)
    s = lax.broadcasted_iota(jnp.int32, (384, 512), 1)
    source = lax.broadcasted_iota(jnp.int32, (384, 512), 0)
    e = s % 16
    chip = (s // 64) % 4 * 8 + (s // 16) % 4 * 2 + s // 256
    wanted = jnp.where(e < 8, chip * 8 + e, 256 + chip * 4 + e - 8)
    moved = dot_nn(pieces, ((wanted == source) & (e < 12)).astype(BF16))
    slot_id = (moved[0:1] + moved[1:2] * 256.0 + moved[2:3] * 65536.0).astype(jnp.int32)
    empty = lax.broadcasted_iota(jnp.int32, (1, 512), 1) % 16 >= 12
    slot_ids[...] = jnp.broadcast_to(jnp.where(empty, -1, slot_id - v * 4096), (8, 512))

    power = lax.broadcasted_iota(jnp.int32, (16, 128), 0)
    power = jnp.where(power == 0, 1, jnp.where(power == 1, 256, jnp.where(power == 2, 65536, 0)))
    id_col = dot_tn(pieces, power.astype(F32).astype(BF16)).astype(jnp.int32)[:, 0:1]
    later = lax.broadcasted_iota(jnp.int32, (384, 384), 0) < lax.broadcasted_iota(
        jnp.int32, (384, 384), 1
    )
    repeat = jnp.max(
        jnp.where((id_col == ids) & later, 1, 0), axis=0, keepdims=True
    )
    ahead = ((id_col >> 9) == (ids >> 9)) & (ids < id_col) & (repeat == 0)
    place_col = jnp.sum(jnp.where(ahead, 1, 0), axis=1, keepdims=True)
    target = lax.broadcasted_iota(jnp.int32, (384, 128), 1)
    chosen = ((id_col >> 9) == v * 8 + target // PACK) & (place_col == target % PACK)
    row_lane = jnp.max(jnp.where(chosen, id_col & 511, -1), axis=0, keepdims=True)
    for copy in own_cot:
        copy.wait()
    pack[...] = dot_tn(chosen.astype(F32).astype(BF16), cot[...]).reshape(8, PACK, 1024)
    packs[r] = pack[r]
    fullest = jnp.max(place_col, axis=(0, 1), keepdims=True)
    meta[x, zh] = jnp.concatenate(
        [
            src_ids[:, 0:128], src_ids[:, 128:256], tgt_ids[...], tgt_mask[...], tgt_order[...],
            row_lane, jnp.broadcast_to(fullest, (1, 128)), jnp.zeros((1, 128), jnp.int32),
        ],
        axis=0,
    )
    meta_r = [
        same(meta.at[x, zh], dev(x=(x + dx) % 4, zh=(zh + dz) % 2)) for dx, dz in rep_offsets
    ]

    def send_pack(offsets):
        copies = []
        for dx, dz in offsets:
            to_x, to_zh = (x + dx) % 4, (zh + dz) % 2
            copies.append(send(pack.at[to_x * 2 + to_zh], packs.at[r], dev(x=to_x, zh=to_zh)))
        return copies

    packs_x = send_pack(rep_offsets[4:])

    row_512 = lax.broadcasted_iota(jnp.int32, (512, 512), 0)

    def emb_part(b, carry):
        onehot = (slot_ids[0:1, :] == row_512 + b * 512).astype(BF16)
        part = dot_tn(onehot, tab[b])

        @pl.when(b == 0)
        def _():
            acc[...] = part

        @pl.when(b != 0)
        def _():
            acc[...] += part

        return carry

    for copy in tab_copies:
        copy.wait()

    def st_y_of(d):
        return rows(c * 256 + (y + 4 - d) % 4 * 64, 64, 64)

    def hid_8th_of(d):
        return rows(c * 64 + (y + 4 - d) % 4 * 16, 16, 16)

    arrive(st_zs)
    st_ya = [same(st.at[0, x, :, st_y, :], ydev(d)) for d in range(1, 4)]
    st_xb = [same(st.at[1, x, :, st_y, :], xdev(d)) for d in range(1, 4)]
    head_z = send_head(rep_offsets[:4])
    arrive(hid_z)
    hid_x = [same(hid.at[x, :, hid_8th, :], xdev(d)) for d in range(1, 4)]
    arrive(st_ya)
    st_xa = [same(st.at[0, x, :, st_c, :], xdev(d)) for d in range(1, 4)]
    arrive(st_xb)
    st_yb = [same(st.at[1, :, :, st_y, :], ydev(d)) for d in range(1, 4)]
    to_core = [
        same(st.at[0, x, :, st_c, :], dev(c=oc)),
        same(st.at[1, :, :, st_y, :], dev(c=oc)),
    ]
    lax.fori_loop(0, 2, emb_part, 0)
    arrive(hid_x)
    hid_y = [same(hid.at[:, :, hid_8th, :], ydev(d)) for d in range(1, 4)]
    hid_c = [same(hid.at[:, :, hid_8th, :], dev(c=oc))]
    lax.fori_loop(2, 5, emb_part, 0)
    for k, d in enumerate((1, 3, 2)):
        arrive([st_xa[d - 1]])
        to_core.append(same(st.at[0, (x + 4 - d) % 4, :, st_c, :], dev(c=oc)))
        arrive([st_yb[d - 1]])
        to_core.append(same(st.at[1, :, :, st_y_of(d), :], dev(c=oc)))
    for d in (1, 3, 2):
        arrive([hid_y[d - 1]])
        hid_c.append(same(hid.at[:, :, hid_8th_of(d), :], dev(c=oc)))
    lax.fori_loop(5, 8, emb_part, 0)
    emb[...] = acc[...].astype(BF16).reshape(2, 256, 1024)
    emb_cs = [send(emb.at[oc], emb_c, dev(c=oc))]

    k_lane = lax.broadcasted_iota(jnp.int32, (128, 512), 1)
    arrival = (k_lane // 64) % 4 * 32 + (k_lane // 16) % 4 * 8 + k_lane // 256 * 4 + k_lane % 4
    expand[...] = (lax.broadcasted_iota(jnp.int32, (128, 512), 0) == arrival).astype(BF16)
    slot = lax.broadcasted_iota(jnp.int32, (512, 512), 0)
    column = lax.broadcasted_iota(jnp.int32, (512, 512), 1)
    arrive(meta_r)
    arrive(to_core)

    def place(i, carry):
        px, pz = i // 2, i % 2
        order = meta[px, pz]
        order = (order // 4) % 2 * 64 + (order // 32) * 16 + (order // 8) % 4 * 4 + order % 4
        order = dot_nn(order.astype(F32).astype(BF16), expand[...])[4:5].astype(jnp.int32)
        move = ((order == slot % 128) & (column // 4 % 4 == slot // 128)).astype(BF16)
        for half in range(2):
            placed = dot_nn(move, st[half, px, pz]).astype(BF16)
            for j in range(4):
                order_st[half * 4 + j, px, pz] = placed[j * 128 : (j + 1) * 128]
        return carry

    lax.fori_loop(0, 8, place, 0)

    arrive(hid_c)
    own_rows = tab.at[r]

    def student(p, carry):
        slog[p] = dot_nt(own_rows[...], hid[p].reshape(256, 1024))
        return carry

    lax.fori_loop(0, 4, student, 0)
    for p in range(4):
        values = slog[p]
        top = jnp.max(values, axis=0, keepdims=True)
        sstat[0, p : p + 1, :] = top
        sstat[0, 4 + p : 5 + p, :] = jnp.sum(jnp.exp(values - top), axis=0, keepdims=True)

    def share_xc(stat, into):
        return [
            send(stat.at[0], into.at[k], xcdev(dx, dc)) for k, (dx, dc) in enumerate(xc_offsets)
        ]

    def share_y(stat, into):
        return [send(stat.at[1], into.at[d - 1], ydev(d)) for d in range(1, 4)]

    def share_z(stat, into):
        return [send(stat.at[2], into.at[d - 1], zdev(d)) for d in range(1, 8)]

    def merged(copies, stat, level, into):
        arrive(copies)
        return merge(stat[level], [into[k] for k in range(len(copies))])

    sst_1s = share_xc(sstat, sst_1)
    arrive(emb_cs)
    emb[c] = (emb[c].astype(F32) + emb_c[...].astype(F32)).astype(BF16)
    emb_ys = [
        send(emb.at[c, rows(((y + d) % 4) * 64, 64, 64)], emb_y.at[d - 1], ydev(d))
        for d in range(1, 4)
    ]

    def teacher(chunk, first):
        def one(p, carry):
            part = dot_nt(headbuf[chunk], order_st[chunk, p].reshape(256, 256))
            if first:
                tlog[p] = part
            else:
                tlog[p] += part
            return carry

        lax.fori_loop(0, 4, one, 0)

    own_head.wait()
    teacher(r, True)
    sstat[1] = merged(sst_1s, sstat, 0, sst_1)
    sst_2s = share_y(sstat, sst_2)
    for k, d in enumerate(range(1, 4)):
        arrive([head_x[k]])
        teacher(((x + 4 - d) % 4) * 2 + zh, False)
    sstat[2] = merged(sst_2s, sstat, 1, sst_2)
    sst_3s = share_z(sstat, sst_3)
    arrive(emb_ys)
    mine = emb[c, rows(y * 64, 64, 64)].astype(F32)
    for d in range(3):
        mine = mine + emb_y[d].astype(F32)
    emb_2[...] = mine.astype(BF16)
    emb_zs = [
        send(emb_2.at[rows(((zl + d) % 4) * 16, 16, 16)], emb_z.at[d - 1], dev(zl=(zl + d) % 4))
        for d in range(1, 4)
    ]

    student_total = merged(sst_3s, sstat, 2, sst_3)
    student_lse = student_total[0:4] + jnp.log(student_total[4:8])
    mask = jnp.concatenate([meta[i // 2, i % 2, 3:4, :] for i in range(8)], axis=0)
    to_slot = position(lax.broadcasted_iota(jnp.int32, (128, 128), 1)) == lax.broadcasted_iota(
        jnp.int32, (128, 128), 0
    )
    mask = dot_nn(mask.astype(F32).astype(BF16), to_slot.astype(BF16))
    mask = jnp.concatenate(
        [jnp.concatenate([mask[2 * p : 2 * p + 1], mask[2 * p + 1 : 2 * p + 2]], axis=1) for p in range(4)],
        axis=0,
    )
    mask_total = jnp.sum(mask, axis=(0, 1), keepdims=True)
    sstat[3, 0:4, :] = student_lse
    sstat[3, 4:8, :] = mask * (8 * 128) / mask_total

    for k, d in enumerate(range(0, 4)):
        arrive([head_z[k]])
        teacher(((x + 4 - d) % 4) * 2 + oz, False)

    for p in range(4):
        values = tlog[p]
        top = jnp.max(values, axis=0, keepdims=True)
        weights = jnp.exp(values - top)
        tstat[0, p : p + 1, :] = top
        tstat[0, 4 + p : 5 + p, :] = jnp.sum(weights, axis=0, keepdims=True)
        cstat[0, p : p + 1, :] = top
        cstat[0, 4 + p : 5 + p, :] = jnp.sum(weights * (values - slog[p]), axis=0, keepdims=True)
    tst_1s = share_xc(tstat, tst_1)
    tstat[1] = merged(tst_1s, tstat, 0, tst_1)
    tst_2s = share_y(tstat, tst_2)
    tstat[2] = merged(tst_2s, tstat, 1, tst_2)
    tst_3s = share_z(tstat, tst_3)
    total = merged(tst_3s, tstat, 2, tst_3)
    teacher_lse = total[0:4] + jnp.log(total[4:8])
    tstat[3, 0:4, :] = teacher_lse
    tstat[3, 4:8, :] = total[4:8]

    def gradient(p):
        row = pl.ds(p, 1)
        student_prob = jnp.exp(slog[p] - sstat[3, row, :])
        teacher_prob = jnp.exp(tlog[p] - tstat[3, row, :])
        return (sstat[3, pl.ds(4 + p, 1), :] * (student_prob - teacher_prob)).astype(BF16)

    packs_z = send_pack(rep_offsets[:4])
    g_x = []
    for d in range(1, 4):
        p = (x + d) % 4
        gbuf[p] = gradient(p)
        g_x.append(send(gbuf.at[p], gx.at[x], xdev(d)))
    own_grad = gradient(x)
    gbuf[x] = own_grad
    gx[x] = own_grad
    cst_1s = share_xc(cstat, cst_1)

    arrive(emb_zs)
    mine = emb_2[rows(zl * 16, 16, 16)].astype(F32)
    for d in range(3):
        mine = mine + emb_z[d].astype(F32)
    mine = (mine * 32.0).astype(BF16)
    src_out[0] = mine[0:8]
    tgt_out[0] = mine[8:12]

    def hidden_part(k, first):
        part = dot_tn(gx[k], tab[k * 2 + zh]).reshape(2, 2, 64, 1024)
        if first:
            hp[...] = part
        else:
            hp[...] += part

    hidden_part(x, True)
    for d in range(1, 4):
        arrive([g_x[d - 1]])
        hidden_part((x + 4 - d) % 4, False)
    hp_cs = [send(hp.at[:, oc], hp_c, dev(c=oc))]
    cstat[1] = merged(cst_1s, cstat, 0, cst_1)
    cst_2s = share_y(cstat, cst_2)

    def table_part(p, carry):
        part = dot_nn(gbuf[p], hid[p].reshape(256, 1024))

        @pl.when(p == 0)
        def _():
            base[...] = part

        @pl.when(p != 0)
        def _():
            base[...] += part

        return carry

    lax.fori_loop(0, 4, table_part, 0)
    arrive(hp_cs)
    h1[...] = (hp[:, c] + hp_c[...]).reshape(2, 4, 16, 1024)
    h1_ys = [send(h1.at[:, (y + d) % 4], h1_y.at[d - 1], ydev(d)) for d in range(1, 4)]

    cstat[2] = merged(cst_2s, cstat, 1, cst_2)
    cst_3s = share_z(cstat, cst_3)
    arrive(h1_ys)
    mine = h1[:, y]
    for d in range(3):
        mine = mine + h1_y[d]
    for i in range(4):
        h2[:, i] = mine[:, 4 * i : 4 * i + 4]
    h2_zs = []
    for d in range(1, 8):
        to = (z + d) % 8
        h2_zs.append(send(h2.at[to // 4, to % 4], h2_z.at[d - 1], zdev(d)))
    arrive(packs_x)
    arrive(packs_z)
    cross = merged(cst_3s, cstat, 2, cst_3)
    token_kl = cross[4:8] / tstat[3, 4:8, :] - tstat[3, 0:4, :] + sstat[3, 0:4, :]
    weight = sstat[3, 4:8, :]
    kl = jnp.sum(weight * token_kl, axis=(0, 1), keepdims=True) / (8 * 128)
    kl_out[...] = kl
    fullest = [meta[i // 2, i % 2, 6:7, 0:1] for i in range(8)]
    full_out[...] = functools.reduce(jnp.maximum, fullest)
    arrive(h2_zs)
    result = h2[zh, zl]
    for d in range(7):
        result = result + h2_z[d]
    hg_out[0] = result
    for copy in pending:
        copy.wait_send()


def add_packed(base, packs, meta, out):
    r = lax.axis_index("rep")
    owned = jnp.concatenate([meta[i // 2, i % 2, 5:6, :] for i in range(8)], axis=0) + 1
    sub_128 = lax.broadcasted_iota(jnp.int32, (128, 128), 0)
    lane_128 = lax.broadcasted_iota(jnp.int32, (128, 128), 1)
    own_slots = (sub_128 == r * PACK + lane_128 % PACK).astype(F32).astype(BF16)
    owned = dot_nn((owned & 255).astype(F32).astype(BF16), own_slots) + 256.0 * dot_nn(
        (owned >> 8).astype(F32).astype(BF16), own_slots
    )
    owned = jnp.where(sub_128[0:8] == lane_128[0:8] // PACK, owned, 0.0)
    owned = jnp.sum(owned, axis=0, keepdims=True).astype(jnp.int32) - 1
    spread = (owned == lax.broadcasted_iota(jnp.int32, (512, 128), 0)).astype(BF16)
    terms = packs[...].reshape(128, 1024)
    coarse = terms.astype(BF16)
    fine = (terms - coarse.astype(F32)).astype(BF16)
    lookup = dot_nn(spread, coarse) + dot_nn(spread, fine)
    out[...] = (base[...] + lookup * 32.0).astype(BF16)


def add_dense(base, src_cot, tgt_cot, meta, out, cots, total, lsem, ssem, rsem):
    v, r = lax.axis_index("vocab"), lax.axis_index("rep")
    copies = [
        pltpu.make_async_copy(src_cot.at[0], cots.at[r, pl.ds(0, 256)], lsem.at[0]),
        pltpu.make_async_copy(tgt_cot.at[0], cots.at[r, pl.ds(256, 128)], lsem.at[1]),
    ]
    for copy in copies:
        copy.start()
    barrier = pltpu.get_barrier_semaphore()
    peers = [(v, (r + d) % 8) for d in range(1, 8)]
    for peer in peers:
        pl.semaphore_signal(barrier, inc=1, device_id=peer, device_id_type=MESH)
    pl.semaphore_wait(barrier, 7)
    for copy in copies:
        copy.wait()
    sends = []
    for k, peer in enumerate(peers):
        sends.append(
            pltpu.make_async_remote_copy(
                src_ref=cots.at[r], dst_ref=cots.at[r], send_sem=ssem.at[k], recv_sem=rsem.at[k],
                device_id=peer, device_id_type=MESH,
            )
        )
        sends[-1].start()
    for copy in sends:
        copy.wait()
    total[...] = base[...]
    row = lax.broadcasted_iota(jnp.int32, (512, 128), 0) + (v * 4096 + r * 512)

    def one(i, carry):
        ids = meta[i // 2, i % 2]
        onehot = jnp.concatenate(
            [(ids[k : k + 1, :] == row).astype(BF16) for k in range(3)], axis=1
        )
        total[...] += dot_nn(onehot, cots[i]) * 32.0
        return carry

    lax.fori_loop(0, 8, one, 0)
    out[...] = total[...].astype(BF16)


def hand_over(*refs):
    half = len(refs) // 2
    for src, dst in zip(refs[:half], refs[half:]):
        dst[...] = src[...]


def on_device(
    src_ids, tgt_ids, tgt_mask, tgt_order, table, student_hidden, teacher_hidden, teacher_head,
    src_embed_grad, tgt_embed_grad,
):
    vmem = pl.BlockSpec(memory_space=pltpu.VMEM)
    hbm = pl.BlockSpec(memory_space=pl.ANY)

    def scratch(shape, dtype=BF16):
        return pltpu.VMEM(shape, dtype)

    def stats():
        return [
            scratch((4, 8, 256), F32), scratch((7, 8, 256), F32), scratch((3, 8, 256), F32),
            scratch((7, 8, 256), F32),
        ]

    outs = (
        jax.ShapeDtypeStruct((1, 8, 1024), BF16),
        jax.ShapeDtypeStruct((1, 4, 1024), BF16),
        jax.ShapeDtypeStruct((1, 1), F32),
        jax.ShapeDtypeStruct((1, 4, 1024), F32),
    )
    table_out = jax.ShapeDtypeStruct((512, 1024), BF16)
    results = pl.pallas_call(
        kernel,
        name="distill",
        out_shape=outs
        + (
            jax.ShapeDtypeStruct((1, 1), jnp.int32),
            jax.ShapeDtypeStruct((512, 1024), F32),
            jax.ShapeDtypeStruct((8, PACK, 1024), F32),
            jax.ShapeDtypeStruct((4, 2, 8, 128), jnp.int32),
        ),
        in_specs=[hbm, hbm, hbm, hbm, hbm, vmem, vmem, vmem, vmem, vmem],
        out_specs=(vmem,) * 8,
        scratch_shapes=[
            scratch((8, 512, 1024)),
            scratch((8, 512, 256)),
            scratch((128, 1024)),
            scratch((4, 2, 128, 1024)),
            scratch((384, 1024)),
            scratch((8, PACK, 1024), F32),
            scratch((2, 4, 2, 512, 256)),
            scratch((2, 16, 256), F32),
            scratch((128, 512)),
            scratch((8, 512), jnp.int32),
            scratch((8, 4, 2, 128, 256)),
            scratch((4, 512, 256), F32),
            scratch((4, 512, 256), F32),
            scratch((512, 1024), F32),
            scratch((4, 512, 256)),
            scratch((4, 512, 256)),
            scratch((2, 256, 1024)),
            scratch((64, 1024)),
            scratch((256, 1024)),
            scratch((3, 64, 1024)),
            scratch((3, 16, 1024)),
            *stats(),
            *stats(),
            *stats(),
            scratch((2, 2, 64, 1024), F32),
            scratch((2, 64, 1024), F32),
            scratch((2, 4, 16, 1024), F32),
            scratch((3, 2, 16, 1024), F32),
            scratch((2, 4, 4, 1024), F32),
            scratch((7, 4, 1024), F32),
            pltpu.SemaphoreType.DMA((16,)),
            pltpu.SemaphoreType.DMA((144,)),
            pltpu.SemaphoreType.DMA((144,)),
        ],
        compiler_params=pltpu.CompilerParams(
            collective_id=0, has_side_effects=True, vmem_limit_bytes=60 * 2**20
        ),
        cost_estimate=pl.CostEstimate(
            flops=12 * 10**9, bytes_accessed=16 * 2**20, transcendentals=2 * 10**6
        ),
    )(
        teacher_head, table, student_hidden, src_embed_grad, tgt_embed_grad, teacher_hidden,
        src_ids, tgt_ids, tgt_mask, tgt_order,
    )
    *results, fullest, base, packs, meta = results

    def packed_path(base, packs, meta):
        return pl.pallas_call(
            add_packed, name="add_packed", out_shape=table_out, in_specs=[vmem] * 3, out_specs=vmem,
        )(base, packs, meta)

    def dense_path(base, packs, meta):
        return pl.pallas_call(
            add_dense,
            name="add_dense",
            out_shape=table_out,
            in_specs=[vmem, hbm, hbm, vmem],
            out_specs=vmem,
            scratch_shapes=[
                scratch((8, 384, 1024)),
                scratch((512, 1024), F32),
                pltpu.SemaphoreType.DMA((2,)),
                pltpu.SemaphoreType.DMA((7,)),
                pltpu.SemaphoreType.DMA((7,)),
            ],
            compiler_params=pltpu.CompilerParams(
                collective_id=1, has_side_effects=True, vmem_limit_bytes=40 * 2**20
            ),
        )(base, src_embed_grad, tgt_embed_grad, meta)

    table_grad = lax.cond(fullest[0, 0] < PACK, packed_path, dense_path, base, packs, meta)
    src, tgt, kl, hidden_grad = pl.pallas_call(
        hand_over, name="hand_over", out_shape=outs, in_specs=[vmem] * 4, out_specs=(vmem,) * 4
    )(*results)
    return (src, tgt, kl[0, 0], hidden_grad, table_grad)


def solution(mesh):
    return jax.shard_map(
        on_device,
        mesh=mesh,
        in_specs=(
            P("rep", None),
            P("rep", None),
            P("rep", None),
            P("rep", None),
            P("vocab", None),
            P("rep", None, None),
            P("rep", "vocab", None),
            P("vocab", "rep"),
            P("rep", None, None),
            P("rep", None, None),
        ),
        out_specs=(
            P("rep", "vocab", None),
            P("rep", "vocab", None),
            P(),
            P("rep", "vocab", None),
            P(("vocab", "rep"), None),
        ),
        check_vma=False,
    )
```

time: 186 us -> 138 us (0.74)
  Pallas kernels: 167 us -> 134 us
  local copies, waits for them, and re-layouts: 13 us -> 0.98 us
  other arithmetic: 5.41 us -> 0 us
    pallas_call x1 -> x3, Pallas kernels: 167 us -> 134 us  [the longest x1 130 us: on_device(): pl.pallas_call(kernel, name='distill', out_shape=outs + (jax.ShapeDtypeSt...]
    unnamed x3, local copies, waits for them, and re-layouts: 4.1 us -> 0.98 us
    broadcast_in_dim x5 -> x0, local copies, waits for them, and re-layouts: 2.83 us -> none  [the longest x2 2.64 us: on_device(): return (emb[None, 0:8], emb[None, 8:12], kl[0, 0], hg[None], tg)]
    unnamed x2 -> x0, other arithmetic: 2.63 us -> none
    reshape x5 -> x0, local copies, waits for them, and re-layouts: 2.47 us -> none  [the longest x1 0.89 us: on_device(): ids_col = jnp.concatenate([slots(src_ids[0], 8) - first_row, slots(tgt_id...]
    another operation x8 -> x0, local copies, waits for them, and re-layouts: 2.14 us -> none  [the longest x6 1.39 us: slots(): values.reshape((4, 4, 2, n) + values.shape[1:]).swapaxes(1, 2)]
where the time goes in v2:
time: 138 us; the launch traced here: 136 us
  Pallas kernels  134 us (97%)
    pallas_call x1, Pallas kernels, on_device(): pl.pallas_call(kernel, name='distill', out_shape=outs + (jax.ShapeDtypeSt...  130 us

profile of v2, /device:TPU:32, one launch (start us, length us, event | category | flops | bytes accessed | tf_op | source)
XLA Modules:
  0.0 136.4 jit_solution(856806396450884555)
XLA Ops:
  0.6 0.0 copy-start
  0.6 130.3 %distill.1 = (bf16[1,8,1024]{2,1,0:T(8,128)(2,1)}, bf16[1,4,1024]{2,1,0:T(4,128)(2,1)}, f32[1,1]{1,0:T(1,128)}, f32[1,4,1024]{2,1,0:T(4,128)}, s32[1,1]{1,0:T(1,...) custom-call(bf16[4096,256]{1,0:T(8,128)(2,1)} %head.1, ...), custom_call_target="tpu_custom_call" | custom-call | flops 12000000000 | bytes 16777216 | tf_op jit(solution)/shard_map/distill/pallas_call | solution.py:569
  131.6 2.0 %hand_over.1 = (bf16[1,8,1024]{2,1,0:T(8,128)(2,1)}, bf16[1,4,1024]{2,1,0:T(4,128)(2,1)}, f32[1,1]{1,0:T(1,128)}, f32[1,4,1024]{2,1,0:T(4,128)}) custom-call(bf16[1,8,1024]{2,1,0:T(8,128)(2,1)} %get-tuple-element.41.refs_0_, bf16[1,4,1024]{2,1,0:T(4,128)(2,1)} %get-tuple-element.42.refs_1_, f32[1,1]{1,0:T(1,128)} %get-tuple-element.43.refs_2_, ...), custom_call_target="tpu_custom_call" | custom-call | tf_op jit(solution)/shard_map/hand_over/pallas_call | solution.py:653
  133.6 0.0 copy-done
  133.6 1.9 %conditional.1 = (bf16[512,1024]{1,0:T(8,128)(2,1)S(1)}) conditional(s32[]{:T(128)} %bitcast.1, (f32[512,1024]{1,0:T(8,128)S(1)}, bf16[1,256,1024]{2,1,0:T(8,128)(2,1)}, bf16[1,128,1024]{2,1,0:T(8,128)(2,1)S(1)}, s32[4,2,8,128]{3,2,1,0:T(8,128)S(1)}) %tuple.21, (f32[512,1024]{1,0:T(8,128)S(1)}, f32[8,16,1024]{2,1,0:T(8,128)}, ...), branch_computations={%region_0.0_spmd, %region_1.0_spmd} | conditional | bytes 8 | solution.py:652
  133.6 1.9 %add_packed.1 = bf16[512,1024]{1,0:T(8,128)(2,1)S(1)} custom-call(f32[512,1024]{1,0:T(8,128)S(1)} %get-tuple-element.21.base, f32[8,16,1024]{2,1,0:T(8,128)} %get-tuple-element.22.packs, s32[4,2,8,128]{3,2,1,0:T(8,128)S(1)} %get-tuple-element.23.meta), custom_call_target="tpu_custom_call" | custom-call | tf_op jit(solution)/shard_map/cond/branch_1_fun/add_packed/pallas_call | solution.py:629
  135.4 1.0 copy.18
Async XLA Ops:
  0.6 132.9 %copy-start = (bf16[1,128,1024]{2,1,0:T(8,128)(2,1)S(1)}, bf16[1,128,1024]{2,1,0:T(8,128)(2,1)}, u32[]{:S(2)}) copy-start(bf16[1,128,1024]{2,1,0:T(8,128)(2,1)} %tgt_cot.1) | copy-start | bytes 786436

commit v3 on v2

--- a/solution.py
+++ b/solution.py
@@ -41,7 +41,7 @@
 def kernel(
     head, table, hidden_in, src_cot, tgt_cot, states_in, src_ids, tgt_ids, tgt_mask, tgt_order,
     src_out, tgt_out, kl_out, hg_out, full_out, base, packs, meta,
-    tab, headbuf, hid_raw, hid, cot, pack, st, st_f32, expand, slot_ids, order_st, slog, tlog,
+    tab, headbuf, hid_raw, hid, cot, pack, st, st_f32, slot_ids, orders, order_st, slog, tlog,
     acc, gbuf, gx, emb, emb_2, emb_c, emb_y, emb_z,
     sstat, sst_1, sst_2, sst_3, tstat, tst_1, tst_2, tst_3, cstat, cst_1, cst_2, cst_3,
     hp, hp_c, h1, h1_y, h2, h2_z,
@@ -111,8 +111,9 @@
     def rows(start, step, count):
         return pl.ds(pl.multiple_of(start, step), count)
 
+    x_cols = rows(x * 256, 256, 256)
     own_raw = local(hidden_in.at[0], hid_raw)
-    own_head = local(head.at[rows(r * 512, 512, 512)], headbuf.at[r])
+    own_head = local(head.at[rows(r * 512, 512, 512)], headbuf.at[0, :, x_cols])
     own_cot = [
         local(src_cot.at[0], cot.at[pl.ds(0, 256)]),
         local(tgt_cot.at[0], cot.at[pl.ds(256, 128)]),
@@ -149,11 +150,31 @@
         for dx, dz in offsets:
             to_x, to_zh = (x + dx) % 4, (zh + dz) % 2
             block = head.at[rows((to_x * 2 + to_zh) * 512, 512, 512)]
-            copies.append(send(block, headbuf.at[r], dev(x=to_x, zh=to_zh)))
+            copies.append(send(block, headbuf.at[dz, :, x_cols], dev(x=to_x, zh=to_zh)))
         return copies
 
+
+    def st_y_of(d):
+        return rows(c * 256 + (y + 4 - d) % 4 * 64, 64, 64)
+
+    def hid_8th_of(d):
+        return rows(c * 64 + (y + 4 - d) % 4 * 16, 16, 16)
+
+    arrive(st_zs)
+    st_ya = [same(st.at[0, x, :, st_y, :], ydev(d)) for d in range(1, 4)]
+    st_xb = [same(st.at[1, x, :, st_y, :], xdev(d)) for d in range(1, 4)]
+    head_z = send_head(rep_offsets[:4])
+    arrive(hid_z)
+    hid_x = [same(hid.at[x, :, hid_8th, :], xdev(d)) for d in range(1, 4)]
+    arrive(st_ya)
+    st_xa = [same(st.at[0, x, :, st_c, :], xdev(d)) for d in range(1, 4)]
+    arrive(st_xb)
+    st_yb = [same(st.at[1, :, :, st_y, :], ydev(d)) for d in range(1, 4)]
     head_x = send_head(rep_offsets[4:])
-
+    to_core = [
+        same(st.at[0, x, :, st_c, :], dev(c=oc)),
+        same(st.at[1, :, :, st_y, :], dev(c=oc)),
+    ]
     ids = jnp.concatenate([src_ids[...], tgt_ids[...]], axis=1)
     pieces = jnp.concatenate(
         [ids & 255, (ids >> 8) & 255, ids >> 16, jnp.zeros((13, 384), jnp.int32)], axis=0
@@ -164,13 +185,14 @@
     chip = (s // 64) % 4 * 8 + (s // 16) % 4 * 2 + s // 256
     wanted = jnp.where(e < 8, chip * 8 + e, 256 + chip * 4 + e - 8)
     moved = dot_nn(pieces, ((wanted == source) & (e < 12)).astype(BF16))
-    slot_id = (moved[0:1] + moved[1:2] * 256.0 + moved[2:3] * 65536.0).astype(jnp.int32)
-    empty = lax.broadcasted_iota(jnp.int32, (1, 512), 1) % 16 >= 12
-    slot_ids[...] = jnp.broadcast_to(jnp.where(empty, -1, slot_id - v * 4096), (8, 512))
-
     power = lax.broadcasted_iota(jnp.int32, (16, 128), 0)
     power = jnp.where(power == 0, 1, jnp.where(power == 1, 256, jnp.where(power == 2, 65536, 0)))
-    id_col = dot_tn(pieces, power.astype(F32).astype(BF16)).astype(jnp.int32)[:, 0:1]
+    power = power.astype(F32).astype(BF16)
+    slot_id = dot_tn(moved.astype(BF16), power).astype(jnp.int32) - v * 4096
+    empty = lax.broadcasted_iota(jnp.int32, (512, 128), 0) % 16 >= 12
+    slot_ids[...] = jnp.where(empty, -1, slot_id)
+
+    id_col = dot_tn(pieces, power).astype(jnp.int32)[:, 0:1]
     later = lax.broadcasted_iota(jnp.int32, (384, 384), 0) < lax.broadcasted_iota(
         jnp.int32, (384, 384), 1
     )
@@ -207,11 +229,11 @@
 
     packs_x = send_pack(rep_offsets[4:])
 
-    row_512 = lax.broadcasted_iota(jnp.int32, (512, 512), 0)
+    row_lane_512 = lax.broadcasted_iota(jnp.int32, (512, 512), 1)
 
     def emb_part(b, carry):
-        onehot = (slot_ids[0:1, :] == row_512 + b * 512).astype(BF16)
-        part = dot_tn(onehot, tab[b])
+        onehot = (slot_ids[:, 0:1] - b * 512 == row_lane_512).astype(BF16)
+        part = dot_nn(onehot, tab[b])
 
         @pl.when(b == 0)
         def _():
@@ -225,32 +247,10 @@
 
     for copy in tab_copies:
         copy.wait()
-
-    def st_y_of(d):
-        return rows(c * 256 + (y + 4 - d) % 4 * 64, 64, 64)
-
-    def hid_8th_of(d):
-        return rows(c * 64 + (y + 4 - d) % 4 * 16, 16, 16)
-
-    arrive(st_zs)
-    st_ya = [same(st.at[0, x, :, st_y, :], ydev(d)) for d in range(1, 4)]
-    st_xb = [same(st.at[1, x, :, st_y, :], xdev(d)) for d in range(1, 4)]
-    head_z = send_head(rep_offsets[:4])
-    arrive(hid_z)
-    hid_x = [same(hid.at[x, :, hid_8th, :], xdev(d)) for d in range(1, 4)]
-    arrive(st_ya)
-    st_xa = [same(st.at[0, x, :, st_c, :], xdev(d)) for d in range(1, 4)]
-    arrive(st_xb)
-    st_yb = [same(st.at[1, :, :, st_y, :], ydev(d)) for d in range(1, 4)]
-    to_core = [
-        same(st.at[0, x, :, st_c, :], dev(c=oc)),
-        same(st.at[1, :, :, st_y, :], dev(c=oc)),
-    ]
-    lax.fori_loop(0, 2, emb_part, 0)
+    lax.fori_loop(0, 1, emb_part, 0)
     arrive(hid_x)
     hid_y = [same(hid.at[:, :, hid_8th, :], ydev(d)) for d in range(1, 4)]
     hid_c = [same(hid.at[:, :, hid_8th, :], dev(c=oc))]
-    lax.fori_loop(2, 5, emb_part, 0)
     for k, d in enumerate((1, 3, 2)):
         arrive([st_xa[d - 1]])
         to_core.append(same(st.at[0, (x + 4 - d) % 4, :, st_c, :], dev(c=oc)))
@@ -259,31 +259,44 @@
     for d in (1, 3, 2):
         arrive([hid_y[d - 1]])
         hid_c.append(same(hid.at[:, :, hid_8th_of(d), :], dev(c=oc)))
-    lax.fori_loop(5, 8, emb_part, 0)
-    emb[...] = acc[...].astype(BF16).reshape(2, 256, 1024)
-    emb_cs = [send(emb.at[oc], emb_c, dev(c=oc))]
 
     k_lane = lax.broadcasted_iota(jnp.int32, (128, 512), 1)
     arrival = (k_lane // 64) % 4 * 32 + (k_lane // 16) % 4 * 8 + k_lane // 256 * 4 + k_lane % 4
-    expand[...] = (lax.broadcasted_iota(jnp.int32, (128, 512), 0) == arrival).astype(BF16)
-    slot = lax.broadcasted_iota(jnp.int32, (512, 512), 0)
-    column = lax.broadcasted_iota(jnp.int32, (512, 512), 1)
+    expand = (lax.broadcasted_iota(jnp.int32, (128, 512), 0) == arrival).astype(BF16)
     arrive(meta_r)
+    order = jnp.concatenate([meta[i // 2, i % 2, 4:5, :] for i in range(8)], axis=0)
+    order = (order // 4) % 2 * 64 + (order // 32) * 16 + (order // 8) % 4 * 4 + order % 4
+    orders[...] = dot_nn(order.astype(F32).astype(BF16), expand).astype(jnp.int32)
+    slot = lax.broadcasted_iota(jnp.int32, (128, 512), 0)
+    part = lax.broadcasted_iota(jnp.int32, (128, 512), 1) // 4 % 4
     arrive(to_core)
 
     def place(i, carry):
         px, pz = i // 2, i % 2
-        order = meta[px, pz]
-        order = (order // 4) % 2 * 64 + (order // 32) * 16 + (order // 8) % 4 * 4 + order % 4
-        order = dot_nn(order.astype(F32).astype(BF16), expand[...])[4:5].astype(jnp.int32)
-        move = ((order == slot % 128) & (column // 4 % 4 == slot // 128)).astype(BF16)
+        order = orders[pl.ds(i, 1), :]
+        hit = jnp.where(order == slot, part, -1)
+        move = jnp.concatenate([(hit == j).astype(BF16) for j in range(4)], axis=0)
         for half in range(2):
             placed = dot_nn(move, st[half, px, pz]).astype(BF16)
             for j in range(4):
-                order_st[half * 4 + j, px, pz] = placed[j * 128 : (j + 1) * 128]
+                block = half * 4 + j
+                order_st[
+                    (zh + block) % 2, px, pz, :, block // 2 * 256 : block // 2 * 256 + 256
+                ] = placed[j * 128 : (j + 1) * 128]
         return carry
 
     lax.fori_loop(0, 8, place, 0)
+
+    def teacher(half, p):
+        return dot_nt(headbuf[half], order_st[half, p].reshape(256, 1024))
+
+    def teacher_near(p, carry):
+        tlog[p] = teacher(0, p)
+        return carry
+
+    own_head.wait()
+    arrive(head_x)
+    lax.fori_loop(0, 4, teacher_near, 0)
 
     arrive(hid_c)
     own_rows = tab.at[r]
@@ -315,33 +328,77 @@
         return merge(stat[level], [into[k] for k in range(len(copies))])
 
     sst_1s = share_xc(sstat, sst_1)
+    lax.fori_loop(1, 8, emb_part, 0)
+    emb[...] = acc[...].astype(BF16).reshape(2, 256, 1024)
+    emb_cs = [send(emb.at[oc], emb_c, dev(c=oc))]
+    sstat[1] = merged(sst_1s, sstat, 0, sst_1)
+    sst_2s = share_y(sstat, sst_2)
+
+    arrive(head_z)
+    packs_z = send_pack(rep_offsets[:4])
+
+    for p in range(4):
+        values = tlog[p] + teacher(1, p)
+        tlog[p] = values
+        top = jnp.max(values, axis=0, keepdims=True)
+        tstat[0, p : p + 1, :] = top
+        tstat[0, 4 + p : 5 + p, :] = jnp.sum(jnp.exp(values - top), axis=0, keepdims=True)
+    tst_1s = share_xc(tstat, tst_1)
+    for p in range(4):
+        values = tlog[p]
+        top = tstat[0, p : p + 1, :]
+        cstat[0, p : p + 1, :] = top
+        cstat[0, 4 + p : 5 + p, :] = jnp.sum(
+            jnp.exp(values - top) * (values - slog[p]), axis=0, keepdims=True
+        )
+    sstat[2] = merged(sst_2s, sstat, 1, sst_2)
+    sst_3s = share_z(sstat, sst_3)
+    tstat[1] = merged(tst_1s, tstat, 0, tst_1)
+    tst_2s = share_y(tstat, tst_2)
     arrive(emb_cs)
     emb[c] = (emb[c].astype(F32) + emb_c[...].astype(F32)).astype(BF16)
     emb_ys = [
         send(emb.at[c, rows(((y + d) % 4) * 64, 64, 64)], emb_y.at[d - 1], ydev(d))
         for d in range(1, 4)
     ]
-
-    def teacher(chunk, first):
-        def one(p, carry):
-            part = dot_nt(headbuf[chunk], order_st[chunk, p].reshape(256, 256))
-            if first:
-                tlog[p] = part
-            else:
-                tlog[p] += part
-            return carry
-
-        lax.fori_loop(0, 4, one, 0)
-
-    own_head.wait()
-    teacher(r, True)
-    sstat[1] = merged(sst_1s, sstat, 0, sst_1)
-    sst_2s = share_y(sstat, sst_2)
-    for k, d in enumerate(range(1, 4)):
-        arrive([head_x[k]])
-        teacher(((x + 4 - d) % 4) * 2 + zh, False)
-    sstat[2] = merged(sst_2s, sstat, 1, sst_2)
-    sst_3s = share_z(sstat, sst_3)
+    tstat[2] = merged(tst_2s, tstat, 1, tst_2)
+    tst_3s = share_z(tstat, tst_3)
+    student_total = merged(sst_3s, sstat, 2, sst_3)
+    student_lse = student_total[0:4] + jnp.log(student_total[4:8])
+    mask = jnp.concatenate([meta[i // 2, i % 2, 3:4, :] for i in range(8)], axis=0)
+    to_slot = position(lax.broadcasted_iota(jnp.int32, (128, 128), 1)) == lax.broadcasted_iota(
+        jnp.int32, (128, 128), 0
+    )
+    mask = dot_nn(mask.astype(F32).astype(BF16), to_slot.astype(BF16))
+    mask = jnp.concatenate(
+        [jnp.concatenate([mask[2 * p : 2 * p + 1], mask[2 * p + 1 : 2 * p + 2]], axis=1) for p in range(4)],
+        axis=0,
+    )
+    mask_total = jnp.sum(mask, axis=(0, 1), keepdims=True)
+    sstat[3, 0:4, :] = student_lse
+    sstat[3, 4:8, :] = mask * (8 * 128) / mask_total
+
+    total = merged(tst_3s, tstat, 2, tst_3)
+    teacher_lse = total[0:4] + jnp.log(total[4:8])
+    tstat[3, 0:4, :] = teacher_lse
+    tstat[3, 4:8, :] = total[4:8]
+
+    def gradient(p):
+        row = pl.ds(p, 1)
+        student_prob = jnp.exp(slog[p] - sstat[3, row, :])
+        teacher_prob = jnp.exp(tlog[p] - tstat[3, row, :])
+        return (sstat[3, pl.ds(4 + p, 1), :] * (student_prob - teacher_prob)).astype(BF16)
+
+    g_x = []
+    for d in range(1, 4):
+        p = (x + d) % 4
+        gbuf[p] = gradient(p)
+        g_x.append(send(gbuf.at[p], gx.at[x], xdev(d)))
+    own_grad = gradient(x)
+    gbuf[x] = own_grad
+    gx[x] = own_grad
+    cst_1s = share_xc(cstat, cst_1)
+
     arrive(emb_ys)
     mine = emb[c, rows(y * 64, 64, 64)].astype(F32)
     for d in range(3):
@@ -352,60 +409,63 @@
         for d in range(1, 4)
     ]
 
-    student_total = merged(sst_3s, sstat, 2, sst_3)
-    student_lse = student_total[0:4] + jnp.log(student_total[4:8])
-    mask = jnp.concatenate([meta[i // 2, i % 2, 3:4, :] for i in range(8)], axis=0)
-    to_slot = position(lax.broadcasted_iota(jnp.int32, (128, 128), 1)) == lax.broadcasted_iota(
-        jnp.int32, (128, 128), 0
-    )
-    mask = dot_nn(mask.astype(F32).astype(BF16), to_slot.astype(BF16))
-    mask = jnp.concatenate(
-        [jnp.concatenate([mask[2 * p : 2 * p + 1], mask[2 * p + 1 : 2 * p + 2]], axis=1) for p in range(4)],
-        axis=0,
-    )
-    mask_total = jnp.sum(mask, axis=(0, 1), keepdims=True)
-    sstat[3, 0:4, :] = student_lse
-    sstat[3, 4:8, :] = mask * (8 * 128) / mask_total
-
-    for k, d in enumerate(range(0, 4)):
-        arrive([head_z[k]])
-        teacher(((x + 4 - d) % 4) * 2 + oz, False)
-
-    for p in range(4):
-        values = tlog[p]
-        top = jnp.max(values, axis=0, keepdims=True)
-        weights = jnp.exp(values - top)
-        tstat[0, p : p + 1, :] = top
-        tstat[0, 4 + p : 5 + p, :] = jnp.sum(weights, axis=0, keepdims=True)
-        cstat[0, p : p + 1, :] = top
-        cstat[0, 4 + p : 5 + p, :] = jnp.sum(weights * (values - slog[p]), axis=0, keepdims=True)
-    tst_1s = share_xc(tstat, tst_1)
-    tstat[1] = merged(tst_1s, tstat, 0, tst_1)
-    tst_2s = share_y(tstat, tst_2)
-    tstat[2] = merged(tst_2s, tstat, 1, tst_2)
-    tst_3s = share_z(tstat, tst_3)
-    total = merged(tst_3s, tstat, 2, tst_3)
-    teacher_lse = total[0:4] + jnp.log(total[4:8])
-    tstat[3, 0:4, :] = teacher_lse
-    tstat[3, 4:8, :] = total[4:8]
-
-    def gradient(p):
-        row = pl.ds(p, 1)
-        student_prob = jnp.exp(slog[p] - sstat[3, row, :])
-        teacher_prob = jnp.exp(tlog[p] - tstat[3, row, :])
-        return (sstat[3, pl.ds(4 + p, 1), :] * (student_prob - teacher_prob)).astype(BF16)
-
-    packs_z = send_pack(rep_offsets[:4])
-    g_x = []
-    for d in range(1, 4):
-        p = (x + d) % 4
-        gbuf[p] = gradient(p)
-        g_x.append(send(gbuf.at[p], gx.at[x], xdev(d)))
-    own_grad = gradient(x)
-    gbuf[x] = own_grad
-    gx[x] = own_grad
-    cst_1s = share_xc(cstat, cst_1)
-
+    def hidden_part(k, half, first):
+        tokens = gx[k, :, half * 128 : half * 128 + 128]
+        product = dot_tn(tokens, tab[k * 2 + zh]).reshape(2, 64, 1024)
+        if first:
+            hp[half] = product
+        else:
+            hp[half] += product
+
+    hp_cs = []
+    for d in range(4):
+        if d > 0:
+            arrive([g_x[d - 1]])
+        for half in range(2):
+            hidden_part((x + 4 - d) % 4, half, d == 0)
+            if d == 3:
+                hp_cs.append(send(hp.at[half, oc], hp_c.at[half], dev(c=oc)))
+    cstat[1] = merged(cst_1s, cstat, 0, cst_1)
+    cst_2s = share_y(cstat, cst_2)
+
+    def table_part(p, carry):
+        part = dot_nn(gbuf[p], hid[p].reshape(256, 1024))
+
+        @pl.when(p == 0)
+        def _():
+            base[...] = part
+
+        @pl.when(p != 0)
+        def _():
+            base[...] += part
+
+        return carry
+
+    lax.fori_loop(0, 4, table_part, 0)
+    h1_ys = []
+    for half in range(2):
+        arrive([hp_cs[half]])
+        h1[half] = (hp[half, c] + hp_c[half]).reshape(4, 16, 1024)
+        h1_ys.append(
+            [
+                send(h1.at[half, (y + d) % 4], h1_y.at[d - 1, half], ydev(d))
+                for d in range(1, 4)
+            ]
+        )
+
+    cstat[2] = merged(cst_2s, cstat, 1, cst_2)
+    cst_3s = share_z(cstat, cst_3)
+    for half in range(2):
+        arrive(h1_ys[half])
+        mine = h1[half, y]
+        for d in range(3):
+            mine = mine + h1_y[d, half]
+        for i in range(4):
+            h2[half, i] = mine[4 * i : 4 * i + 4]
+    h2_zs = []
+    for d in range(1, 8):
+        to = (z + d) % 8
+        h2_zs.append(send(h2.at[to // 4, to % 4], h2_z.at[d - 1], zdev(d)))
     arrive(emb_zs)
     mine = emb_2[rows(zl * 16, 16, 16)].astype(F32)
     for d in range(3):
@@ -414,51 +474,6 @@
     src_out[0] = mine[0:8]
     tgt_out[0] = mine[8:12]
 
-    def hidden_part(k, first):
-        part = dot_tn(gx[k], tab[k * 2 + zh]).reshape(2, 2, 64, 1024)
-        if first:
-            hp[...] = part
-        else:
-            hp[...] += part
-
-    hidden_part(x, True)
-    for d in range(1, 4):
-        arrive([g_x[d - 1]])
-        hidden_part((x + 4 - d) % 4, False)
-    hp_cs = [send(hp.at[:, oc], hp_c, dev(c=oc))]
-    cstat[1] = merged(cst_1s, cstat, 0, cst_1)
-    cst_2s = share_y(cstat, cst_2)
-
-    def table_part(p, carry):
-        part = dot_nn(gbuf[p], hid[p].reshape(256, 1024))
-
-        @pl.when(p == 0)
-        def _():
-            base[...] = part
-
-        @pl.when(p != 0)
-        def _():
-            base[...] += part
-
-        return carry
-
-    lax.fori_loop(0, 4, table_part, 0)
-    arrive(hp_cs)
-    h1[...] = (hp[:, c] + hp_c[...]).reshape(2, 4, 16, 1024)
-    h1_ys = [send(h1.at[:, (y + d) % 4], h1_y.at[d - 1], ydev(d)) for d in range(1, 4)]
-
-    cstat[2] = merged(cst_2s, cstat, 1, cst_2)
-    cst_3s = share_z(cstat, cst_3)
-    arrive(h1_ys)
-    mine = h1[:, y]
-    for d in range(3):
-        mine = mine + h1_y[d]
-    for i in range(4):
-        h2[:, i] = mine[:, 4 * i : 4 * i + 4]
-    h2_zs = []
-    for d in range(1, 8):
-        to = (z + d) % 8
-        h2_zs.append(send(h2.at[to // 4, to % 4], h2_z.at[d - 1], zdev(d)))
     arrive(packs_x)
     arrive(packs_z)
     cross = merged(cst_3s, cstat, 2, cst_3)
@@ -580,16 +595,16 @@
         out_specs=(vmem,) * 8,
         scratch_shapes=[
             scratch((8, 512, 1024)),
-            scratch((8, 512, 256)),
+            scratch((2, 512, 1024)),
             scratch((128, 1024)),
             scratch((4, 2, 128, 1024)),
             scratch((384, 1024)),
             scratch((8, PACK, 1024), F32),
             scratch((2, 4, 2, 512, 256)),
             scratch((2, 16, 256), F32),
-            scratch((128, 512)),
+            scratch((512, 128), jnp.int32),
             scratch((8, 512), jnp.int32),
-            scratch((8, 4, 2, 128, 256)),
+            scratch((2, 4, 2, 128, 1024)),
             scratch((4, 512, 256), F32),
             scratch((4, 512, 256), F32),
             scratch((512, 1024), F32),

time: 138 us -> 138 us (level)
  no operation moved by 1% of the time
where the time goes in v3:
time: 138 us; the launch traced here: 137 us
  Pallas kernels  134 us (97%)
    pallas_call x1, Pallas kernels, on_device(): pl.pallas_call(kernel, name='distill', out_shape=outs + (jax.ShapeDtypeSt...  130 us

profile of v3, /device:TPU:32, one launch (start us, length us, event | category | flops | bytes accessed | tf_op | source)
XLA Modules:
  0.0 136.6 jit_solution(13585990456519671871)
XLA Ops:
  0.6 0.0 copy-start
  0.6 130.5 %distill.1 = (bf16[1,8,1024]{2,1,0:T(8,128)(2,1)}, bf16[1,4,1024]{2,1,0:T(4,128)(2,1)}, f32[1,1]{1,0:T(1,128)}, f32[1,4,1024]{2,1,0:T(4,128)}, s32[1,1]{1,0:T(1,...) custom-call(bf16[4096,256]{1,0:T(8,128)(2,1)} %head.1, ...), custom_call_target="tpu_custom_call" | custom-call | flops 12000000000 | bytes 16777216 | tf_op jit(solution)/shard_map/distill/pallas_call | solution.py:584
  131.8 2.0 %hand_over.1 = (bf16[1,8,1024]{2,1,0:T(8,128)(2,1)}, bf16[1,4,1024]{2,1,0:T(4,128)(2,1)}, f32[1,1]{1,0:T(1,128)}, f32[1,4,1024]{2,1,0:T(4,128)}) custom-call(bf16[1,8,1024]{2,1,0:T(8,128)(2,1)} %get-tuple-element.41.refs_0_, bf16[1,4,1024]{2,1,0:T(4,128)(2,1)} %get-tuple-element.42.refs_1_, f32[1,1]{1,0:T(1,128)} %get-tuple-element.43.refs_2_, ...), custom_call_target="tpu_custom_call" | custom-call | tf_op jit(solution)/shard_map/hand_over/pallas_call | solution.py:668
  133.8 0.0 copy-done
  133.8 1.9 %conditional.1 = (bf16[512,1024]{1,0:T(8,128)(2,1)S(1)}) conditional(s32[]{:T(128)} %bitcast.1, (f32[512,1024]{1,0:T(8,128)S(1)}, bf16[1,256,1024]{2,1,0:T(8,128)(2,1)}, bf16[1,128,1024]{2,1,0:T(8,128)(2,1)S(1)}, s32[4,2,8,128]{3,2,1,0:T(8,128)S(1)}) %tuple.21, (f32[512,1024]{1,0:T(8,128)S(1)}, f32[8,16,1024]{2,1,0:T(8,128)}, ...), branch_computations={%region_0.0_spmd, %region_1.0_spmd} | conditional | bytes 8 | solution.py:667
  133.8 1.9 %add_packed.1 = bf16[512,1024]{1,0:T(8,128)(2,1)S(1)} custom-call(f32[512,1024]{1,0:T(8,128)S(1)} %get-tuple-element.21.base, f32[8,16,1024]{2,1,0:T(8,128)} %get-tuple-element.22.packs, s32[4,2,8,128]{3,2,1,0:T(8,128)S(1)} %get-tuple-element.23.meta), custom_call_target="tpu_custom_call" | custom-call | tf_op jit(solution)/shard_map/cond/branch_1_fun/add_packed/pallas_call | solution.py:644
  135.7 1.0 copy.18
Async XLA Ops:
  0.6 133.1 %copy-start = (bf16[1,128,1024]{2,1,0:T(8,128)(2,1)S(1)}, bf16[1,128,1024]{2,1,0:T(8,128)(2,1)}, u32[]{:S(2)}) copy-start(bf16[1,128,1024]{2,1,0:T(8,128)(2,1)} %tgt_cot.1) | copy-start | bytes 786436

commit v4 on v3

--- a/solution.py
+++ b/solution.py
@@ -163,13 +163,13 @@
     arrive(st_zs)
     st_ya = [same(st.at[0, x, :, st_y, :], ydev(d)) for d in range(1, 4)]
     st_xb = [same(st.at[1, x, :, st_y, :], xdev(d)) for d in range(1, 4)]
-    head_z = send_head(rep_offsets[:4])
     arrive(hid_z)
     hid_x = [same(hid.at[x, :, hid_8th, :], xdev(d)) for d in range(1, 4)]
     arrive(st_ya)
     st_xa = [same(st.at[0, x, :, st_c, :], xdev(d)) for d in range(1, 4)]
     arrive(st_xb)
     st_yb = [same(st.at[1, :, :, st_y, :], ydev(d)) for d in range(1, 4)]
+    head_z = send_head(rep_offsets[:4])
     head_x = send_head(rep_offsets[4:])
     to_core = [
         same(st.at[0, x, :, st_c, :], dev(c=oc)),

time: 138 us -> 141 us (1.022)
  Pallas kernels: 134 us -> 137 us
    pallas_call x1, Pallas kernels: 130 us -> 134 us  [on_device(): pl.pallas_call(kernel, name='distill', out_shape=outs + (jax.ShapeDtypeSt...]
where the time goes in v4:
time: 141 us; the launch traced here: 140 us
  Pallas kernels  137 us (97%)
    pallas_call x1, Pallas kernels, on_device(): pl.pallas_call(kernel, name='distill', out_shape=outs + (jax.ShapeDtypeSt...  134 us

profile of v4, /device:TPU:32, one launch (start us, length us, event | category | flops | bytes accessed | tf_op | source)
XLA Modules:
  0.0 139.7 jit_solution(10493439476532757882)
XLA Ops:
  0.6 0.0 copy-start
  0.6 133.5 %distill.1 = (bf16[1,8,1024]{2,1,0:T(8,128)(2,1)}, bf16[1,4,1024]{2,1,0:T(4,128)(2,1)}, f32[1,1]{1,0:T(1,128)}, f32[1,4,1024]{2,1,0:T(4,128)}, s32[1,1]{1,0:T(1,...) custom-call(bf16[4096,256]{1,0:T(8,128)(2,1)} %head.1, ...), custom_call_target="tpu_custom_call" | custom-call | flops 12000000000 | bytes 16777216 | tf_op jit(solution)/shard_map/distill/pallas_call | solution.py:584
  134.8 2.0 %hand_over.1 = (bf16[1,8,1024]{2,1,0:T(8,128)(2,1)}, bf16[1,4,1024]{2,1,0:T(4,128)(2,1)}, f32[1,1]{1,0:T(1,128)}, f32[1,4,1024]{2,1,0:T(4,128)}) custom-call(bf16[1,8,1024]{2,1,0:T(8,128)(2,1)} %get-tuple-element.41.refs_0_, bf16[1,4,1024]{2,1,0:T(4,128)(2,1)} %get-tuple-element.42.refs_1_, f32[1,1]{1,0:T(1,128)} %get-tuple-element.43.refs_2_, ...), custom_call_target="tpu_custom_call" | custom-call | tf_op jit(solution)/shard_map/hand_over/pallas_call | solution.py:668
  136.8 0.0 copy-done
  136.8 1.9 %conditional.1 = (bf16[512,1024]{1,0:T(8,128)(2,1)S(1)}) conditional(s32[]{:T(128)} %bitcast.1, (f32[512,1024]{1,0:T(8,128)S(1)}, bf16[1,256,1024]{2,1,0:T(8,128)(2,1)}, bf16[1,128,1024]{2,1,0:T(8,128)(2,1)S(1)}, s32[4,2,8,128]{3,2,1,0:T(8,128)S(1)}) %tuple.21, (f32[512,1024]{1,0:T(8,128)S(1)}, f32[8,16,1024]{2,1,0:T(8,128)}, ...), branch_computations={%region_0.0_spmd, %region_1.0_spmd} | conditional | bytes 8 | solution.py:667
  136.8 1.9 %add_packed.1 = bf16[512,1024]{1,0:T(8,128)(2,1)S(1)} custom-call(f32[512,1024]{1,0:T(8,128)S(1)} %get-tuple-element.21.base, f32[8,16,1024]{2,1,0:T(8,128)} %get-tuple-element.22.packs, s32[4,2,8,128]{3,2,1,0:T(8,128)S(1)} %get-tuple-element.23.meta), custom_call_target="tpu_custom_call" | custom-call | tf_op jit(solution)/shard_map/cond/branch_1_fun/add_packed/pallas_call | solution.py:644
  138.7 1.0 copy.18
Async XLA Ops:
  0.6 136.2 %copy-start = (bf16[1,128,1024]{2,1,0:T(8,128)(2,1)S(1)}, bf16[1,128,1024]{2,1,0:T(8,128)(2,1)}, u32[]{:S(2)}) copy-start(bf16[1,128,1024]{2,1,0:T(8,128)(2,1)} %tgt_cot.1) | copy-start | bytes 786436
